TPU v7x, 128 devices: a whole 4x4x4 slice. The times are simulated.
128 devices in a mesh: actor: 4 (over z_lo, core), learn: 32 (over z_hi, x, y).
Axes of the slice: x: 4, y: 4, z: 4 (z_hi: 2, z_lo: 2; z = z_hi * 2 + z_lo), core: 2. Of those that a mesh axis runs over, the one named last changes fastest.
Arguments:
- rec_weight: bfloat16 [2048, 4, 2048], P('learn', None, 'actor'), may hold values from -0.4375 to 0.4375
- head_weight: bfloat16 [2048, 128], P('learn'), may hold values from -0.125 to 0.125
- value_head: bfloat16 [2048], P('learn'), may hold values from -0.25 to 0.25
- gate_inputs: bfloat16 [32, 64, 16, 4, 2048], P('learn', None, None, None, 'actor'), may hold values from -3 to 3
- start_state: bfloat16 [32, 64, 2, 2048], P('learn', None, None, 'actor'), may hold values from -3 to 3
- advantages: bfloat16 [32, 64, 16], P('learn'), may hold values from -6 to 6
- returns: bfloat16 [32, 64, 16], P('learn'), may hold values from -6 to 6
- old_logprob: bfloat16 [32, 64, 16], P('learn'), may hold values from -5.375 to -4.28125
- taken_action: int32 [32, 64, 16], P('learn'), may hold values from 0 to 127
- episode_start: int32 [32, 64, 16], P('learn'), may hold values 0 or 1
- segment_counts: int32 [32], replicated, may hold values from 1 to 64, 1024 in all
- assignment: int32 [32, 64], P('learn'), may hold values from 0 to 31, as said below
Outputs:
- grad_rec: float32 [2048, 4, 2048], P('learn', None, 'actor')
- grad_policy: float32 [2048, 128], P('learn')
- grad_value: float32 [2048], P('learn')
- learner_values: float32 [32, 64, 16], P('learn')
Inputs may be any that keep to these rules, and one draw needn't show every extreme that they name: `segment_counts`: only slots below a group's count hold live segments; the counts sum to 1024 and the largest equals 64. `assignment`: each group's row names every learner exactly 2 times.
All inputs are finite; a program needn't handle non-finite values. No bound on the sum of `episode_start` on one device may be relied on, other than what follows from the above.
Results may differ from a plain program's by a relative error of at most 0.038.
Values may be sent and summed in bfloat16 or wider, within the bound.
A program may use at most 128 MiB of HBM per device.

v0:
```python
import jax
import jax.numpy as jnp
from jax import lax
from jax.sharding import PartitionSpec as P

penalty_weight = 0.5


def cell_gates(preact):
    in_gate = jax.nn.sigmoid(preact[:, 0])
    forget = jax.nn.sigmoid(preact[:, 1])
    candidate = jnp.tanh(preact[:, 2])
    out_gate = jax.nn.sigmoid(preact[:, 3])
    return (in_gate, forget, candidate, out_gate)


def cell_backward(preact, kept_cell, grad_hidden, grad_cell):
    in_gate, forget, candidate, out_gate = cell_gates(preact)
    squash = jnp.tanh(forget * kept_cell + in_gate * candidate)
    grad_out = grad_hidden * squash
    grad_total = grad_cell + grad_hidden * out_gate * (1.0 - squash * squash)
    grad_pre = jnp.stack(
        [
            grad_total * candidate * in_gate * (1.0 - in_gate),
            grad_total * kept_cell * forget * (1.0 - forget),
            grad_total * in_gate * (1.0 - candidate * candidate),
            grad_out * out_gate * (1.0 - out_gate),
        ],
        axis=1,
    ).astype(jnp.bfloat16)
    return (grad_pre, grad_total * forget)


def head_terms(
    hidden_rows, head_weight, value_head, chosen_action, advantage, target, old_value, weight
):
    logits = jnp.dot(hidden_rows, head_weight, preferred_element_type=jnp.float32)
    logsoft = jax.nn.log_softmax(logits, axis=-1)
    onehot = (lax.broadcasted_iota(jnp.int32, logits.shape, 1) == chosen_action[:, None]).astype(
        jnp.float32
    )
    chosen = jnp.sum(logsoft * onehot, axis=1)
    ratio = jnp.exp(chosen - old_value)
    estimate = jnp.dot(hidden_rows, value_head, preferred_element_type=jnp.float32)
    grad_ratio = (-ratio * advantage + penalty_weight * (ratio - 1.0)) * weight
    grad_logits = (grad_ratio[:, None] * (onehot - jnp.exp(logsoft))).astype(jnp.bfloat16)
    grad_estimate = ((estimate - target) * weight).astype(jnp.bfloat16)
    return (estimate, grad_logits, grad_estimate)


def flatten(values_in):
    return values_in.T.reshape(-1)


def train(rec_full, head_full, value_full, gate_in, state_in, floats, integers, live):
    width_full = rec_full.shape[0]
    quarter = rec_full.shape[2]
    batch_size = gate_in.shape[0]
    step_count = gate_in.shape[1]
    rec_matrix = rec_full.reshape(width_full, 4 * quarter)
    offset = lax.axis_index("actor") * quarter
    inputs = jnp.transpose(gate_in, (1, 0, 2, 3))
    keep_masks = (1 - integers[:, 1]).astype(jnp.float32).T
    hidden_start = lax.all_gather(state_in[:, 0], "actor", axis=1, tiled=True)
    cell_start = state_in[:, 1].astype(jnp.float32)

    def advance(state_pair, slice_in):
        hidden_prev, cell_prev = state_pair
        step_input, keep_now = slice_in
        kept_hidden = hidden_prev * keep_now.astype(jnp.bfloat16)[:, None]
        kept_cell = cell_prev * keep_now[:, None]
        preact = step_input.astype(jnp.float32) + jnp.dot(
            kept_hidden, rec_matrix, preferred_element_type=jnp.float32
        ).reshape(step_input.shape)
        in_gate, forget, candidate, out_gate = cell_gates(preact)
        cell_new = forget * kept_cell + in_gate * candidate
        hidden_part = (out_gate * jnp.tanh(cell_new)).astype(jnp.bfloat16)
        hidden_new = lax.all_gather(hidden_part, "actor", axis=1, tiled=True)
        return ((hidden_new, cell_new), (kept_hidden, kept_cell, preact, hidden_new))

    final_pair, saved = lax.scan(advance, (hidden_start, cell_start), (inputs, keep_masks))
    kept_hidden, kept_cell, preact, hidden = saved
    hidden_rows = hidden.reshape(step_count * batch_size, width_full)
    weight = jnp.broadcast_to(
        live.astype(jnp.float32)[None, :] / step_count, (step_count, batch_size)
    ).reshape(-1)
    estimate, grad_logits, grad_estimate = head_terms(
        hidden_rows,
        head_full,
        value_full,
        flatten(integers[:, 0]),
        flatten(floats[:, 0]).astype(jnp.float32),
        flatten(floats[:, 1]).astype(jnp.float32),
        flatten(floats[:, 2]).astype(jnp.float32),
        weight,
    )
    head_part = lax.dynamic_slice_in_dim(head_full, offset, quarter, 0)
    value_part = lax.dynamic_slice_in_dim(value_full, offset, quarter, 0)
    head_hidden = (
        jnp.dot(grad_logits, head_part.T, preferred_element_type=jnp.float32)
        + grad_estimate.astype(jnp.float32)[:, None] * value_part.astype(jnp.float32)[None, :]
    ).reshape(step_count, batch_size, quarter)

    def retreat(state_pair, slice_in):
        grad_hidden, grad_cell = state_pair
        preact_step, kept_step, keep_now, head_step = slice_in
        grad_pre, grad_cell_prev = cell_backward(
            preact_step, kept_step, head_step + grad_hidden, grad_cell
        )
        partial_sum = jnp.dot(
            grad_pre.reshape(batch_size, -1), rec_matrix.T, preferred_element_type=jnp.float32
        )
        grad_prev = (
            lax.psum_scatter(
                partial_sum.astype(jnp.bfloat16), "actor", scatter_dimension=1, tiled=True
            ).astype(jnp.float32)
            * keep_now[:, None]
        )
        return ((grad_prev, grad_cell_prev * keep_now[:, None]), grad_pre)

    blank = jnp.zeros((batch_size, quarter), jnp.float32)
    back_pair, grad_pres = lax.scan(
        retreat, (blank, blank), (preact, kept_cell, keep_masks, head_hidden), reverse=True
    )
    rec_grad = jnp.dot(
        kept_hidden.reshape(step_count * batch_size, width_full).T,
        grad_pres.reshape(step_count * batch_size, 4 * quarter),
        preferred_element_type=jnp.float32,
    ).reshape(width_full, 4, quarter)
    head_grad = jnp.dot(hidden_rows.T, grad_logits, preferred_element_type=jnp.float32)
    value_grad = jnp.dot(grad_estimate, hidden_rows, preferred_element_type=jnp.float32)
    estimates = estimate.reshape(step_count, batch_size).T * live.astype(jnp.float32)[:, None]
    return (rec_grad, head_grad, value_grad, estimates)


def shards(
    rec_weight,
    head_weight,
    value_head,
    gate_inputs,
    start_state,
    advantages,
    returns,
    old_logprob,
    taken_action,
    episode_start,
    segment_counts,
    assignment,
):
    learners = lax.axis_size("learn")
    batch_size = gate_inputs.shape[1]
    per_pair = batch_size // learners
    rec_full, head_full, value_full = (
        lax.all_gather(rec_weight, "learn", axis=0, tiled=True),
        lax.all_gather(head_weight, "learn", axis=0, tiled=True),
        lax.all_gather(value_head, "learn", axis=0, tiled=True),
    )
    position = lax.axis_index("learn")
    lanes = jnp.arange(learners, dtype=jnp.int32)
    own_count = jnp.sum(jnp.where(lanes == position, segment_counts, 0))
    live_here = (jnp.arange(batch_size, dtype=jnp.int32) < own_count).astype(jnp.int32)
    slot_order = jnp.argsort(assignment[0], stable=True)
    floats = jnp.stack([advantages[0], returns[0], old_logprob[0]], axis=1)
    integers = jnp.stack([taken_action[0], episode_start[0]], axis=1)

    def arrange(values_in):
        return jnp.take(values_in, slot_order, axis=0).reshape(
            (learners, per_pair) + values_in.shape[1:]
        )

    def unfold(values_in):
        return values_in.reshape((batch_size,) + values_in.shape[2:])

    gate_moved, state_moved, float_moved, integer_moved, live_moved = (
        lax.all_to_all(arrange(gate_inputs[0]), "learn", split_axis=0, concat_axis=0, tiled=True),
        lax.all_to_all(arrange(start_state[0]), "learn", split_axis=0, concat_axis=0, tiled=True),
        lax.all_to_all(arrange(floats), "learn", split_axis=0, concat_axis=0, tiled=True),
        lax.all_to_all(arrange(integers), "learn", split_axis=0, concat_axis=0, tiled=True),
        lax.all_to_all(arrange(live_here), "learn", split_axis=0, concat_axis=0, tiled=True),
    )
    rec_grad, head_grad, value_grad, estimates = train(
        rec_full,
        head_full,
        value_full,
        unfold(gate_moved),
        unfold(state_moved),
        unfold(float_moved),
        unfold(integer_moved),
        unfold(live_moved),
    )
    rec_share, head_share, value_share = (
        lax.psum_scatter(
            rec_grad.astype(jnp.bfloat16), "learn", scatter_dimension=0, tiled=True
        ).astype(jnp.float32),
        lax.psum_scatter(
            head_grad.astype(jnp.bfloat16), "learn", scatter_dimension=0, tiled=True
        ).astype(jnp.float32),
        lax.psum_scatter(
            value_grad.astype(jnp.bfloat16), "learn", scatter_dimension=0, tiled=True
        ).astype(jnp.float32),
    )
    return (rec_share, head_share, value_share, estimates[None])


def solution(mesh):
    placed = (
        P("learn", None, "actor"),
        P("learn", None),
        P("learn"),
        P("learn", None, None, None, "actor"),
        P("learn", None, None, "actor"),
        P("learn", None, None),
        P("learn", None, None),
        P("learn", None, None),
        P("learn", None, None),
        P("learn", None, None),
        P(),
        P("learn", None),
    )
    return jax.shard_map(
        shards,
        mesh=mesh,
        in_specs=placed,
        out_specs=(P("learn", None, "actor"), P("learn", None), P("learn"), P("learn", None, None)),
        check_vma=False,
    )
```

profile of v0, /device:TPU:0, one launch (start us, length us, event | category | flops | bytes accessed | tf_op | source)
XLA Modules:
  0.0 1517.2 jit_solution(8931885861530432225)
XLA Ops:
  14.1 10.7 all-to-all-start.4
  40.2 8.2 all-to-all-done.3
  63.7 9.9 all-to-all-start
  84.7 7.5 all-to-all-start.1
  93.8 140.5 %all-reduce = bf16[2048]{0:T(1024)(128)(2,1)S(1)} all-reduce(bf16[2048]{0:T(1024)(128)(2,1)S(1)} %dynamic-update-slice), channel_id=1, replica_groups=mesh['actor'=4,'learn'=32] {'learn'}, use_global_device_ids=true, to_apply=%add | all-reduce | flops 2048 | bytes 8192
  234.4 90.2 %all_gather.17 = bf16[2048,128]{1,0:T(8,128)(2,1)S(1)} all-gather(bf16[64,128]{1,0:T(8,128)(2,1)S(1)} %copy-done.3), channel_id=1, replica_groups=mesh['actor'=4,'learn'=32] {'learn'}, dimensions={0}, use_global_device_ids=true | all-gather | bytes 540672 | tf_op jit(solution)/shard_map/all_gather | solution.py:155
  325.8 8.5 all-gather
  344.0 10.2 copy.170
  354.2 280.7 %while.39 = (s32[]{:T(128)}, bf16[64,2048]{1,0:T(8,128)(2,1)S(1)}, f32[64,512]{1,0:T(8,128)S(1)}, bf16[16,64,2048]{2,1,0:T(8,128)(2,1)}, f32[16,64,512]{2,1,0:T(...) while((s32[]{:T(128)}, bf16[64,2048]{1,0:T(8,128)(2,1)S(1)}, ...), condition=%wide.region_2.3_spmd, body=%wide.region_1.2_spmd.sunk | while | flops 538574912 | bytes 17698292 | solution.py:81
  363.1 5.9 all_gather.20
  647.8 471.4 %while.40 = (s32[]{:T(128)}, f32[64,512]{1,0:T(8,128)S(1)}, f32[64,512]{1,0:T(8,128)S(1)}, bf16[16,64,4,512]{3,2,1,0:T(4,128)(2,1)}, f32[16,64,512]{2,1,0:T(8,12...) while((s32[]{:T(128)}, f32[64,512]{1,0:T(8,128)S(1)}, ...), condition=%wide.region_9.10_spmd.clone, body=%wide.region_7.9_spmd.clone.sunk | while | flops 539590656 | bytes 17171656 | solution.py:122
  651.5 6.7 convolution_convert_fusion.4
  659.2 12.4 reduce-scatter.8.cloned.1.call-done
  676.3 6.7 convolution_convert_fusion.4
  684.0 17.5 %reduce-scatter.8.cloned.1.call-done = bf16[64,512]{1,0:T(8,128)(2,1)} async-done(((bf16[64,2048]{1,0:T(8,128)(2,1)}), bf16[64,512]{1,0:T(8,128)(2,1)}) %reduce-scatter.8.cloned.1.call-update) | async-done | bytes 65552 | tf_op jit(solution)/shard_map/while/body/eval_jaxpr/reduce_scatter | solution.py:114
  706.1 6.7 convolution_convert_fusion.4
  713.8 17.5 %reduce-scatter.8.cloned.1.call-done = bf16[64,512]{1,0:T(8,128)(2,1)} async-done(((bf16[64,2048]{1,0:T(8,128)(2,1)}), bf16[64,512]{1,0:T(8,128)(2,1)}) %reduce-scatter.8.cloned.1.call-update) | async-done | bytes 65552 | tf_op jit(solution)/shard_map/while/body/eval_jaxpr/reduce_scatter | solution.py:114
  735.9 6.7 convolution_convert_fusion.4
  743.7 17.4 %reduce-scatter.8.cloned.1.call-done = bf16[64,512]{1,0:T(8,128)(2,1)} async-done(((bf16[64,2048]{1,0:T(8,128)(2,1)}), bf16[64,512]{1,0:T(8,128)(2,1)}) %reduce-scatter.8.cloned.1.call-update) | async-done | bytes 65552 | tf_op jit(solution)/shard_map/while/body/eval_jaxpr/reduce_scatter | solution.py:114
  765.7 6.7 convolution_convert_fusion.4
  773.4 17.4 %reduce-scatter.8.cloned.1.call-done = bf16[64,512]{1,0:T(8,128)(2,1)} async-done(((bf16[64,2048]{1,0:T(8,128)(2,1)}), bf16[64,512]{1,0:T(8,128)(2,1)}) %reduce-scatter.8.cloned.1.call-update) | async-done | bytes 65552 | tf_op jit(solution)/shard_map/while/body/eval_jaxpr/reduce_scatter | solution.py:114
  795.5 6.7 convolution_convert_fusion.4
  803.2 17.4 %reduce-scatter.8.cloned.1.call-done = bf16[64,512]{1,0:T(8,128)(2,1)} async-done(((bf16[64,2048]{1,0:T(8,128)(2,1)}), bf16[64,512]{1,0:T(8,128)(2,1)}) %reduce-scatter.8.cloned.1.call-update) | async-done | bytes 65552 | tf_op jit(solution)/shard_map/while/body/eval_jaxpr/reduce_scatter | solution.py:114
  825.2 6.7 convolution_convert_fusion.4
  833.0 17.4 %reduce-scatter.8.cloned.1.call-done = bf16[64,512]{1,0:T(8,128)(2,1)} async-done(((bf16[64,2048]{1,0:T(8,128)(2,1)}), bf16[64,512]{1,0:T(8,128)(2,1)}) %reduce-scatter.8.cloned.1.call-update) | async-done | bytes 65552 | tf_op jit(solution)/shard_map/while/body/eval_jaxpr/reduce_scatter | solution.py:114
  855.0 6.7 convolution_convert_fusion.4
  862.7 17.4 %reduce-scatter.8.cloned.1.call-done = bf16[64,512]{1,0:T(8,128)(2,1)} async-done(((bf16[64,2048]{1,0:T(8,128)(2,1)}), bf16[64,512]{1,0:T(8,128)(2,1)}) %reduce-scatter.8.cloned.1.call-update) | async-done | bytes 65552 | tf_op jit(solution)/shard_map/while/body/eval_jaxpr/reduce_scatter | solution.py:114
  884.8 6.7 convolution_convert_fusion.4
  892.5 17.4 %reduce-scatter.8.cloned.1.call-done = bf16[64,512]{1,0:T(8,128)(2,1)} async-done(((bf16[64,2048]{1,0:T(8,128)(2,1)}), bf16[64,512]{1,0:T(8,128)(2,1)}) %reduce-scatter.8.cloned.1.call-update) | async-done | bytes 65552 | tf_op jit(solution)/shard_map/while/body/eval_jaxpr/reduce_scatter | solution.py:114
  914.6 6.7 convolution_convert_fusion.4
  922.3 17.4 %reduce-scatter.8.cloned.1.call-done = bf16[64,512]{1,0:T(8,128)(2,1)} async-done(((bf16[64,2048]{1,0:T(8,128)(2,1)}), bf16[64,512]{1,0:T(8,128)(2,1)}) %reduce-scatter.8.cloned.1.call-update) | async-done | bytes 65552 | tf_op jit(solution)/shard_map/while/body/eval_jaxpr/reduce_scatter | solution.py:114
  944.3 6.7 convolution_convert_fusion.4
  952.0 17.4 %reduce-scatter.8.cloned.1.call-done = bf16[64,512]{1,0:T(8,128)(2,1)} async-done(((bf16[64,2048]{1,0:T(8,128)(2,1)}), bf16[64,512]{1,0:T(8,128)(2,1)}) %reduce-scatter.8.cloned.1.call-update) | async-done | bytes 65552 | tf_op jit(solution)/shard_map/while/body/eval_jaxpr/reduce_scatter | solution.py:114
  974.1 6.7 convolution_convert_fusion.4
  981.8 17.4 %reduce-scatter.8.cloned.1.call-done = bf16[64,512]{1,0:T(8,128)(2,1)} async-done(((bf16[64,2048]{1,0:T(8,128)(2,1)}), bf16[64,512]{1,0:T(8,128)(2,1)}) %reduce-scatter.8.cloned.1.call-update) | async-done | bytes 65552 | tf_op jit(solution)/shard_map/while/body/eval_jaxpr/reduce_scatter | solution.py:114
  1003.9 6.7 convolution_convert_fusion.4
  1011.6 17.4 %reduce-scatter.8.cloned.1.call-done = bf16[64,512]{1,0:T(8,128)(2,1)} async-done(((bf16[64,2048]{1,0:T(8,128)(2,1)}), bf16[64,512]{1,0:T(8,128)(2,1)}) %reduce-scatter.8.cloned.1.call-update) | async-done | bytes 65552 | tf_op jit(solution)/shard_map/while/body/eval_jaxpr/reduce_scatter | solution.py:114
  1033.6 6.7 convolution_convert_fusion.4
  1041.4 17.4 %reduce-scatter.8.cloned.1.call-done = bf16[64,512]{1,0:T(8,128)(2,1)} async-done(((bf16[64,2048]{1,0:T(8,128)(2,1)}), bf16[64,512]{1,0:T(8,128)(2,1)}) %reduce-scatter.8.cloned.1.call-update) | async-done | bytes 65552 | tf_op jit(solution)/shard_map/while/body/eval_jaxpr/reduce_scatter | solution.py:114
  1063.4 6.7 convolution_convert_fusion.4
  1071.1 17.4 %reduce-scatter.8.cloned.1.call-done = bf16[64,512]{1,0:T(8,128)(2,1)} async-done(((bf16[64,2048]{1,0:T(8,128)(2,1)}), bf16[64,512]{1,0:T(8,128)(2,1)}) %reduce-scatter.8.cloned.1.call-update) | async-done | bytes 65552 | tf_op jit(solution)/shard_map/while/body/eval_jaxpr/reduce_scatter | solution.py:114
  1093.2 6.7 convolution_convert_fusion.4
  1100.9 17.4 %reduce-scatter.8.cloned.1.call-done = bf16[64,512]{1,0:T(8,128)(2,1)} async-done(((bf16[64,2048]{1,0:T(8,128)(2,1)}), bf16[64,512]{1,0:T(8,128)(2,1)}) %reduce-scatter.8.cloned.1.call-update) | async-done | bytes 65552 | tf_op jit(solution)/shard_map/while/body/eval_jaxpr/reduce_scatter | solution.py:114
  1125.6 6.4 copy.159
  1132.0 14.1 convolution_convert_fusion.1
  1149.7 96.1 %all-reduce.1 = bf16[2048]{0:T(1024)(128)(2,1)S(1)} all-reduce(bf16[2048]{0:T(1024)(128)(2,1)S(1)} %convert_element_type.196), channel_id=6, replica_groups=mesh['actor'=4,'learn'=32] {'learn'}, use_global_device_ids=true, to_apply=%region_12.13.clone | all-reduce | flops 2048 | bytes 8192
  1247.0 61.0 %reduce-scatter.6.cloned.1.call-done = bf16[64,128]{1,0:T(8,128)(2,1)} async-done(((bf16[2048,128]{1,0:T(8,128)(2,1)}), bf16[64,128]{1,0:T(8,128)(2,1)}) %reduce-scatter.6.cloned.1.call-update) | async-done | bytes 16400 | tf_op jit(solution)/shard_map/reduce_scatter | solution.py:195
  1309.3 199.2 %reduce-scatter.4.cloned.1.call-done = bf16[64,4,512]{2,0,1:T(8,128)(2,1)} async-done(((bf16[2048,4,512]{2,0,1:T(8,128)(2,1)}), bf16[64,4,512]{2,0,1:T(8,128)(2,1)}) %reduce-scatter.4.cloned.1.call-update) | async-done | bytes 262160 | tf_op jit(solution)/shard_map/reduce_scatter | solution.py:192
  (522 shorter events, 449.5 us)
Async XLA Ops:
  7.2 32.2 %copy-start = (bf16[1,64,2,512]{3,2,1,0:T(2,128)(2,1)S(1)}, bf16[1,64,2,512]{3,2,1,0:T(2,128)(2,1)}, u32[]{:S(2)}) copy-start(bf16[1,64,2,512]{3,2,1,0:T(2,128)(2,1)} %param.20) | copy-start | bytes 393220
  7.2 336.8 %all-gather.3.cloned.1.call-start = ((), (), s32[]{:S(2)}) async-start(), calls=%async_computation.8 | async-start | bytes 8650752 | tf_op jit(solution)/shard_map/all_gather | solution.py:154
  14.1 20.4 %all-to-all-start.4 = ((s32[32,1,2]{2,1,0:T(1,128)}), s32[32,1,2]{2,1,0:T(1,128)S(1)}, u32[]{:S(2)}, u32[]{:S(2)}) async-start(s32[32,1,2]{2,1,0:T(1,128)} %bitcast.35), calls=%async_computation.5 | async-start | bytes 32768 | tf_op jit(solution)/shard_map/all_to_all | solution.py:179
  34.5 13.9 all-to-all-start.3
  48.4 15.3 %all-to-all-start.2 = ((s32[32,2,2,16]{3,1,2,0:T(2,128)}), s32[32,2,2,16]{3,1,2,0:T(2,128)S(1)}, u32[]{:S(2)}, u32[]{:S(2)}) async-start(s32[32,2,2,16]{3,1,2,0:T(2,128)} %copy.138), calls=%async_computation.3 | async-start | bytes 131072 | tf_op jit(solution)/shard_map/all_to_all | solution.py:178
  63.7 21.0 %all-to-all-start = ((bf16[32,2,2,512]{3,1,2,0:T(2,128)(2,1)}), bf16[32,2,2,512]{3,1,2,0:T(2,128)(2,1)S(1)}, u32[]{:S(2)}, u32[]{:S(2)}) async-start(bf16[32,2,2,512]{3,1,2,0:T(2,128)(2,1)} %copy.131), calls=%async_computation.1 | async-start | bytes 262144 | tf_op jit(solution)/shard_map/all_to_all | solution.py:176
  82.1 10.2 copy-start.4
  82.1 11.5 copy-start.5
  82.1 152.3 %copy-start.3 = (bf16[64,128]{1,0:T(8,128)(2,1)S(1)}, bf16[64,128]{1,0:T(8,128)(2,1)}, u32[]{:S(2)}) copy-start(bf16[64,128]{1,0:T(8,128)(2,1)} %param.17) | copy-start | bytes 49156
  84.7 249.8 %all-to-all-start.1 = ((bf16[32,2,16,4,512]{4,3,1,2,0:T(4,128)(2,1)}), bf16[32,2,16,4,512]{4,3,1,2,0:T(4,128)(2,1)}, u32[]{:S(2)}, u32[]{:S(2)}) async-start(bf16[32,2,16,4,512]{4,3,1,2,0:T(4,128)(2,1)} %copy.134), calls=%async_computation.2 | async-start | bytes 8388608 | tf_op jit(solution)/shard_map/all_to_all | solution.py:175
  634.9 4.0 copy-start.2
  647.8 23.8 %reduce-scatter.8.cloned.1.call-start = ((), (), s32[]{:S(2)}) async-start(), calls=%async_computation.11 | async-start | bytes 327680 | tf_op jit(solution)/shard_map/while/body/eval_jaxpr/reduce_scatter | solution.py:114
  672.6 28.9 %reduce-scatter.8.cloned.1.call-start = ((), (), s32[]{:S(2)}) async-start(), calls=%async_computation.11 | async-start | bytes 327680 | tf_op jit(solution)/shard_map/while/body/eval_jaxpr/reduce_scatter | solution.py:114
  702.4 28.9 %reduce-scatter.8.cloned.1.call-start = ((), (), s32[]{:S(2)}) async-start(), calls=%async_computation.11 | async-start | bytes 327680 | tf_op jit(solution)/shard_map/while/body/eval_jaxpr/reduce_scatter | solution.py:114
  732.2 28.8 %reduce-scatter.8.cloned.1.call-start = ((), (), s32[]{:S(2)}) async-start(), calls=%async_computation.11 | async-start | bytes 327680 | tf_op jit(solution)/shard_map/while/body/eval_jaxpr/reduce_scatter | solution.py:114
  762.0 28.8 %reduce-scatter.8.cloned.1.call-start = ((), (), s32[]{:S(2)}) async-start(), calls=%async_computation.11 | async-start | bytes 327680 | tf_op jit(solution)/shard_map/while/body/eval_jaxpr/reduce_scatter | solution.py:114
  791.8 28.8 %reduce-scatter.8.cloned.1.call-start = ((), (), s32[]{:S(2)}) async-start(), calls=%async_computation.11 | async-start | bytes 327680 | tf_op jit(solution)/shard_map/while/body/eval_jaxpr/reduce_scatter | solution.py:114
  821.5 28.8 %reduce-scatter.8.cloned.1.call-start = ((), (), s32[]{:S(2)}) async-start(), calls=%async_computation.11 | async-start | bytes 327680 | tf_op jit(solution)/shard_map/while/body/eval_jaxpr/reduce_scatter | solution.py:114
  851.3 28.8 %reduce-scatter.8.cloned.1.call-start = ((), (), s32[]{:S(2)}) async-start(), calls=%async_computation.11 | async-start | bytes 327680 | tf_op jit(solution)/shard_map/while/body/eval_jaxpr/reduce_scatter | solution.py:114
  881.1 28.8 %reduce-scatter.8.cloned.1.call-start = ((), (), s32[]{:S(2)}) async-start(), calls=%async_computation.11 | async-start | bytes 327680 | tf_op jit(solution)/shard_map/while/body/eval_jaxpr/reduce_scatter | solution.py:114
  910.8 28.8 %reduce-scatter.8.cloned.1.call-start = ((), (), s32[]{:S(2)}) async-start(), calls=%async_computation.11 | async-start | bytes 327680 | tf_op jit(solution)/shard_map/while/body/eval_jaxpr/reduce_scatter | solution.py:114
  940.6 28.8 %reduce-scatter.8.cloned.1.call-start = ((), (), s32[]{:S(2)}) async-start(), calls=%async_computation.11 | async-start | bytes 327680 | tf_op jit(solution)/shard_map/while/body/eval_jaxpr/reduce_scatter | solution.py:114
  970.4 28.8 %reduce-scatter.8.cloned.1.call-start = ((), (), s32[]{:S(2)}) async-start(), calls=%async_computation.11 | async-start | bytes 327680 | tf_op jit(solution)/shard_map/while/body/eval_jaxpr/reduce_scatter | solution.py:114
  1000.2 28.8 %reduce-scatter.8.cloned.1.call-start = ((), (), s32[]{:S(2)}) async-start(), calls=%async_computation.11 | async-start | bytes 327680 | tf_op jit(solution)/shard_map/while/body/eval_jaxpr/reduce_scatter | solution.py:114
  1029.9 28.8 %reduce-scatter.8.cloned.1.call-start = ((), (), s32[]{:S(2)}) async-start(), calls=%async_computation.11 | async-start | bytes 327680 | tf_op jit(solution)/shard_map/while/body/eval_jaxpr/reduce_scatter | solution.py:114
  1059.7 28.8 %reduce-scatter.8.cloned.1.call-start = ((), (), s32[]{:S(2)}) async-start(), calls=%async_computation.11 | async-start | bytes 327680 | tf_op jit(solution)/shard_map/while/body/eval_jaxpr/reduce_scatter | solution.py:114
  1089.5 28.8 %reduce-scatter.8.cloned.1.call-start = ((), (), s32[]{:S(2)}) async-start(), calls=%async_computation.11 | async-start | bytes 327680 | tf_op jit(solution)/shard_map/while/body/eval_jaxpr/reduce_scatter | solution.py:114
  1119.2 188.7 %reduce-scatter.6.cloned.1.call-start = ((), (), s32[]{:S(2)}) async-start(), calls=%async_computation.10 | async-start | bytes 540672 | tf_op jit(solution)/shard_map/reduce_scatter | solution.py:195
  1119.8 388.7 %reduce-scatter.4.cloned.1.call-start = ((), (), s32[]{:S(2)}) async-start(), calls=%async_computation.9 | async-start | bytes 8650752 | tf_op jit(solution)/shard_map/reduce_scatter | solution.py:192
  1146.1 364.4 %copy-start.1 = (bf16[1,64,2,512]{3,2,1,0:T(2,128)(2,1)S(1)}, bf16[1,64,2,512]{3,2,1,0:T(2,128)(2,1)}, u32[]{:S(2)}) copy-start(bf16[1,64,2,512]{3,2,1,0:T(2,128)(2,1)} %param.20) | copy-start | bytes 393220
Sparse Core Ops, SparseCore 0:
  11.1 154.4 all-gather.2
  658.4 13.1 reduce-scatter.7
  683.2 18.2 reduce-scatter.7
  713.0 18.2 reduce-scatter.7
  742.8 18.1 reduce-scatter.7
  772.6 18.1 reduce-scatter.7
  802.4 18.1 reduce-scatter.7
  832.1 18.1 reduce-scatter.7
  861.9 18.1 reduce-scatter.7
  891.7 18.1 reduce-scatter.7
  921.4 18.1 reduce-scatter.7
  951.2 18.1 reduce-scatter.7
  981.0 18.1 reduce-scatter.7
  1010.8 18.1 reduce-scatter.7
  1040.5 18.1 reduce-scatter.7
  1070.3 18.1 reduce-scatter.7
  1100.1 18.1 reduce-scatter.7
  1122.7 185.2 reduce-scatter.5
  1310.5 197.9 reduce-scatter.3
where the time goes:
time: 1530 us; the launch traced here: 1520 us
  waiting for transfers between devices  552 us (36%)
  blocking collectives  429 us (28%)
  matrix products  214 us (14%)
  other arithmetic  147 us (10%)
  local copies, waits for them, and re-layouts  121 us (8%)
  starting transfers between devices  36.9 us (2%)
  between operations  15.7 us (1%)
    reduce_scatter x16, waiting for transfers between devices, retreat(): lax.psum_scatter(partial_sum.astype(jnp.bfloat16), 'actor', scatter_dimen...  273 us
    unnamed x2, blocking collectives  237 us
    reduce_scatter x1, waiting for transfers between devices, shards(): lax.psum_scatter(rec_grad.astype(jnp.bfloat16), 'learn', scatter_dimensio...  199 us
    dot_general x16, matrix products, retreat(): jnp.dot(grad_pre.reshape(batch_size, -1), rec_matrix.T, preferred_element...  108 us
    all_gather x16, blocking collectives, advance(): hidden_new = lax.all_gather(hidden_part, 'actor', axis=1, tiled=True)  93.6 us
    all_gather x1, blocking collectives, shards(): lax.all_gather(head_weight, 'learn', axis=0, tiled=True)  90.2 us
    dot_general x16, matrix products, advance(): jnp.dot(kept_hidden, rec_matrix, preferred_element_type=jnp.float32)  80 us
    reduce_scatter x1, waiting for transfers between devices, shards(): lax.psum_scatter(head_grad.astype(jnp.bfloat16), 'learn', scatter_dimensi...  61 us
  transfers between devices with their start and end apart: 24, of which 21 were waited for; matrix products, arithmetic and copies ran while one was open for 6% of the time, Pallas kernels for 0%

commit v1 on v0

v1 whole, which is shorter than its diff:
```python
import jax
import jax.numpy as jnp
from jax import lax
from jax.experimental import pallas as pl
from jax.experimental.pallas import tpu as pltpu
from jax.sharding import PartitionSpec as P

MESH = pl.DeviceIdType.MESH
BF = jnp.bfloat16
F32 = jnp.float32
UNITS = 2048
QUARTER = 512
BATCH = 64
STEPS = 16
CHOICES = 128
VMEM = pl.BlockSpec(memory_space=pltpu.VMEM)
LIMIT = 60 * 2**20
OFFSETS = (2, -1, 1, 0)


def params(collective):
    return pltpu.CompilerParams(
        collective_id=collective, has_side_effects=True, vmem_limit_bytes=LIMIT
    )


def meet(devices):
    barrier = pltpu.get_barrier_semaphore()
    for device in devices:
        pl.semaphore_signal(barrier, inc=1, device_id=device, device_id_type=MESH)
    pl.semaphore_wait(barrier, len(devices))


class Torus:
    def __init__(self):
        place = lax.axis_index("learn")
        self.z, self.x, self.y = place // 16, lax.rem(place // 4, 4), lax.rem(place, 4)

    def device(self, dz, dx, dy):
        z = lax.rem(self.z + dz, 2)
        x = lax.rem(self.x + dx + 4, 4)
        y = lax.rem(self.y + dy + 4, 4)
        return {"learn": z * 16 + x * 4 + y}

    def first(self, half, d):
        return self.device(0, d, 0) if half == 0 else self.device(0, 0, d)

    def second(self, half, d):
        return self.device(0, 0, d) if half == 0 else self.device(0, d, 0)

    def other(self):
        return self.device(1, 0, 0)

    def neighbours(self):
        return [
            self.device(0, 1, 0),
            self.device(0, -1, 0),
            self.device(0, 0, 1),
            self.device(0, 0, -1),
            self.other(),
        ]

    def rows(self, half, plane, dp, dq, part=None):
        dx, dy = (dp, dq) if half == 0 else (dq, dp)
        block = self.device(plane, dx, dy)["learn"]
        start = block * 64 + 32 * half
        if part is None:
            return pl.ds(pl.multiple_of(start, 32), 32)
        return pl.ds(pl.multiple_of(start + 16 * part, 16), 16)


def gather_keys():
    keys = []
    for half in (0, 1):
        keys += [("p", half, d) for d in (1, -1)]
        keys += [("pf", half, d) for d in (1, -1)]
        keys += [("z", half, dp) for dp in OFFSETS]
        for plane in (0, 1):
            for dp in OFFSETS:
                keys += [("q", half, plane, dp, d) for d in (1, -1)]
                keys += [("qf", half, plane, dp, d) for d in (1, -1)]
    return {key: index for index, key in enumerate(keys)}


KEYS = gather_keys()


def gather_blocks(held, send_sems, recv_sems):
    torus = Torus()
    started = []

    def move(key, rows, device):
        index = KEYS[key]
        return pltpu.make_async_remote_copy(
            src_ref=held.at[rows],
            dst_ref=held.at[rows],
            send_sem=send_sems.at[index],
            recv_sem=recv_sems.at[index],
            device_id=device,
            device_id_type=MESH,
        )

    def send(key, rows, device):
        copy = move(key, rows, device)
        copy.start()
        started.append(copy)

    def arrive(key, rows):
        move(key, rows, torus.other()).wait_recv()

    def spread(half, plane, dp):
        for d in (1, -1):
            send(("q", half, plane, dp, d), torus.rows(half, plane, dp, 0), torus.second(half, d))

    def pass_on(half, plane, dp):
        for d in (1, -1):
            part = 0 if d == 1 else 1
            arrive(("q", half, plane, dp, d), torus.rows(half, plane, dp, -d))
            send(
                ("qf", half, plane, dp, d),
                torus.rows(half, plane, dp, -d, part),
                torus.second(half, d),
            )

    def cross(half, dp):
        send(("z", half, dp), torus.rows(half, 0, dp, 0), torus.other())

    def crossed(half, dp):
        arrive(("z", half, dp), torus.rows(half, 1, dp, 0))
        spread(half, 1, dp)

    for half in (0, 1):
        for d in (1, -1):
            send(("p", half, d), torus.rows(half, 0, 0, 0), torus.first(half, d))
    for half in (0, 1):
        cross(half, 0)
        spread(half, 0, 0)
    for half in (0, 1):
        for d in (1, -1):
            part = 0 if d == 1 else 1
            arrive(("p", half, d), torus.rows(half, 0, -d, 0))
            send(("pf", half, d), torus.rows(half, 0, -d, 0, part), torus.first(half, d))
            cross(half, -d)
    for half in (0, 1):
        for d in (1, -1):
            spread(half, 0, -d)
    for half in (0, 1):
        crossed(half, 0)
        for d in (1, -1):
            part = 0 if d == 1 else 1
            arrive(("pf", half, d), torus.rows(half, 0, -2 * d, 0, part))
        cross(half, 2)
        spread(half, 0, 2)
    for half in (0, 1):
        pass_on(half, 0, 0)
    for half in (0, 1):
        for d in (1, -1):
            crossed(half, -d)
    for half in (0, 1):
        for d in (1, -1):
            pass_on(half, 0, -d)
    for half in (0, 1):
        crossed(half, 2)
    for half in (0, 1):
        pass_on(half, 1, 0)
    for half in (0, 1):
        pass_on(half, 0, 2)
    for half in (0, 1):
        for d in (1, -1):
            pass_on(half, 1, -d)
    for half in (0, 1):
        pass_on(half, 1, 2)
    for half in (0, 1):
        for plane in (0, 1):
            for dp in OFFSETS:
                for d in (1, -1):
                    part = 0 if d == 1 else 1
                    arrive(
                        ("qf", half, plane, dp, d), torus.rows(half, plane, dp, -2 * d, part)
                    )
    for copy in started:
        copy.wait_send()


def gather_kernel(block_ref, held, send_sems, recv_sems):
    torus = Torus()
    meet(torus.neighbours())
    place = lax.axis_index("learn")
    held[pl.ds(pl.multiple_of(place * 64, 64), 64), :] = block_ref[...]
    gather_blocks(held, send_sems, recv_sems)


def gather_weights(block):
    return pl.pallas_call(
        gather_kernel,
        out_shape=jax.ShapeDtypeStruct((UNITS, block.shape[1]), BF),
        in_specs=[VMEM],
        out_specs=VMEM,
        scratch_shapes=[
            pltpu.SemaphoreType.DMA((len(KEYS),)),
            pltpu.SemaphoreType.DMA((len(KEYS),)),
        ],
        compiler_params=params(1),
        name="gather_weights",
    )(block)


def reduce_kernel(own, out_ref, staged, quarters, halves, send_sems, recv_sems):
    torus = Torus()
    meet(torus.neighbours())
    started = []
    slots = {"qf": 0, "q": 0, "pf": 0, "p": 0, "z": 0}
    where = {}
    for key in KEYS:
        small = key[0] in ("qf", "pf")
        kind = "quarter" if small else "half"
        where[key] = slots.setdefault(kind, 0)
        slots[kind] += 1

    def landing(key):
        size = 16 if key[0] in ("qf", "pf") else 32
        buffer = quarters if size == 16 else halves
        return buffer.at[pl.ds(where[key] * size, size)]

    def send(key, source, device):
        index = KEYS[key]
        copy = pltpu.make_async_remote_copy(
            src_ref=source,
            dst_ref=landing(key),
            send_sem=send_sems.at[index],
            recv_sem=recv_sems.at[index],
            device_id=device,
            device_id_type=MESH,
        )
        copy.start()
        started.append(copy)

    def arrived(key):
        index = KEYS[key]
        ref = landing(key)
        pltpu.make_async_remote_copy(
            src_ref=ref,
            dst_ref=ref,
            send_sem=send_sems.at[index],
            recv_sem=recv_sems.at[index],
            device_id=torus.other(),
            device_id_type=MESH,
        ).wait_recv()
        return ref[...].astype(F32)

    stage = {}

    def slot(key):
        if key not in stage:
            stage[key] = len(stage)
        return staged.at[pl.ds(stage[key] * 32, 32)]

    def far(half, plane, dp):
        for d in (1, -1):
            part = 0 if d == 1 else 1
            send(
                ("qf", half, plane, dp, d),
                own.at[torus.rows(half, plane, dp, -2 * d, part)],
                torus.second(half, -d),
            )

    def near(half, plane, dp):
        for d in (1, -1):
            part = 0 if d == 1 else 1
            target = slot(("q", half, plane, dp, d))
            target[...] = own[torus.rows(half, plane, dp, -d), :]
            extra = arrived(("qf", half, plane, dp, d))
            rows = pl.ds(16 * part, 16)
            target[rows, :] = (target[rows, :].astype(F32) + extra).astype(BF)
            send(("q", half, plane, dp, d), target, torus.second(half, -d))

    def line(half, plane, dp):
        total = own[torus.rows(half, plane, dp, 0), :].astype(F32)
        for d in (1, -1):
            total = total + arrived(("q", half, plane, dp, d))
        return total

    def cross(half, dp):
        target = slot(("z", half, dp))
        target[...] = line(half, 1, dp).astype(BF)
        send(("z", half, dp), target, torus.other())

    def plane_sum(half, dp):
        return line(half, 0, dp) + arrived(("z", half, dp))

    for plane in (1, 0):
        for dp in OFFSETS:
            for half in (0, 1):
                far(half, plane, dp)
    for plane in (1, 0):
        for dp in OFFSETS:
            for half in (0, 1):
                near(half, plane, dp)
    for dp in OFFSETS:
        for half in (0, 1):
            cross(half, dp)
    for half in (0, 1):
        target = slot(("pf", half))
        target[...] = plane_sum(half, 2).astype(BF)
        for d in (1, -1):
            part = 0 if d == 1 else 1
            send(("pf", half, d), target.at[pl.ds(16 * part, 16)], torus.first(half, -d))
    for half in (0, 1):
        for d in (1, -1):
            part = 0 if d == 1 else 1
            target = slot(("p", half, d))
            target[...] = plane_sum(half, -d).astype(BF)
            extra = arrived(("pf", half, d))
            rows = pl.ds(16 * part, 16)
            target[rows, :] = (target[rows, :].astype(F32) + extra).astype(BF)
            send(("p", half, d), target, torus.first(half, -d))
    for half in (0, 1):
        total = plane_sum(half, 0)
        for d in (1, -1):
            total = total + arrived(("p", half, d))
        out_ref[pl.ds(32 * half, 32), :] = total
    for copy in started:
        copy.wait_send()


def reduce_gradient(partial):
    width = partial.shape[1]
    quarters = sum(1 for key in KEYS if key[0] in ("qf", "pf"))
    halves = len(KEYS) - quarters
    return pl.pallas_call(
        reduce_kernel,
        out_shape=jax.ShapeDtypeStruct((64, width), F32),
        in_specs=[VMEM],
        out_specs=VMEM,
        scratch_shapes=[
            pltpu.VMEM((46 * 32, width), BF),
            pltpu.VMEM((quarters * 16, width), BF),
            pltpu.VMEM((halves * 32, width), BF),
            pltpu.SemaphoreType.DMA((len(KEYS),)),
            pltpu.SemaphoreType.DMA((len(KEYS),)),
        ],
        compiler_params=params(2),
        name="reduce_gradient",
    )(partial)


def actor_peers():
    me = lax.axis_index("actor")
    core = me + 1 - 2 * lax.rem(me, 2)
    across = lax.rem(me + 2, 4)
    return me, (core, across, 3 - me)


def columns(quarter):
    return pl.ds(pl.multiple_of(quarter * QUARTER, QUARTER), QUARTER)


def sigmoid(value):
    return 0.5 * jnp.tanh(0.5 * value) + 0.5


def forward_kernel(
    weight_ref, gate_ref, keep_ref, state_ref, hidden, factors, preact, cell, send_sems, recv_sems
):
    me, peers = actor_peers()
    meet([{"actor": peer} for peer in peers])

    def copies(t):
        result = []
        for index, peer in enumerate(peers):
            part = hidden.at[t, :, columns(me)]
            result.append(
                pltpu.make_async_remote_copy(
                    src_ref=part,
                    dst_ref=part,
                    send_sem=send_sems.at[t, index],
                    recv_sem=recv_sems.at[t, index],
                    device_id={"actor": peer},
                    device_id_type=MESH,
                )
            )
        return result

    def arrive(t, index):
        part = hidden.at[t, :, columns(peers[index])]
        pltpu.make_async_remote_copy(
            src_ref=part,
            dst_ref=part,
            send_sem=send_sems.at[t, index],
            recv_sem=recv_sems.at[t, index],
            device_id={"actor": peers[index]},
            device_id_type=MESH,
        ).wait_recv()

    def multiply(t, quarter, first):
        part = hidden[t, :, columns(quarter)]
        for k in range(4):
            spot = pl.ds(k * QUARTER, QUARTER)
            product = jnp.dot(
                part, weight_ref[columns(quarter), spot], preferred_element_type=F32
            )
            if first:
                preact[:, spot] = product
            else:
                preact[:, spot] += product

    def start(t):
        sends = copies(t)
        sends[1].start()
        sends[2].start()
        sends[0].start()

    hidden[0, :, columns(me)] = state_ref[:, 0:QUARTER]
    start(0)
    cell[...] = state_ref[:, QUARTER:].astype(F32)

    def step(t, carry):
        multiply(t, me, True)
        for index in range(3):
            arrive(t, index)
            multiply(t, peers[index], False)
        for chunk in range(QUARTER // 128):
            spot = pl.ds(chunk * 128, 128)
            keep = keep_ref[t]
            kept = keep * cell[:, spot]
            gates = []
            for k in range(4):
                wide = pl.ds(k * QUARTER + chunk * 128, 128)
                gates.append(gate_ref[t, :, wide].astype(F32) + keep * preact[:, wide])
            inp = sigmoid(gates[0])
            forget = sigmoid(gates[1])
            cand = jnp.tanh(gates[2])
            outg = sigmoid(gates[3])
            new_cell = forget * kept + inp * cand
            squash = jnp.tanh(new_cell)
            cell[:, spot] = new_cell
            part = pl.ds(pl.multiple_of(me * QUARTER + chunk * 128, 128), 128)
            hidden[t + 1, :, part] = (outg * squash).astype(BF)
            held = (
                outg * (1.0 - squash * squash),
                keep * cand * inp * (1.0 - inp),
                kept * forget * (1.0 - forget),
                keep * inp * (1.0 - cand * cand),
                keep * squash * outg * (1.0 - outg),
                keep * forget,
            )
            for index, value in enumerate(held):
                factors[t, index, :, spot] = value.astype(BF)
        start(t + 1)
        for copy in copies(t):
            copy.wait_send()
        return carry

    lax.fori_loop(0, STEPS, step, 0)
    for index in range(3):
        arrive(STEPS, index)
    for copy in copies(STEPS):
        copy.wait_send()


def forward(weight, gates, keep, state):
    return pl.pallas_call(
        forward_kernel,
        out_shape=(
            jax.ShapeDtypeStruct((STEPS + 1, BATCH, UNITS), BF),
            jax.ShapeDtypeStruct((STEPS, 6, BATCH, QUARTER), BF),
        ),
        in_specs=[VMEM] * 4,
        out_specs=(VMEM, VMEM),
        scratch_shapes=[
            pltpu.VMEM((BATCH, UNITS), F32),
            pltpu.VMEM((BATCH, QUARTER), F32),
            pltpu.SemaphoreType.DMA((STEPS + 1, 3)),
            pltpu.SemaphoreType.DMA((STEPS + 1, 3)),
        ],
        compiler_params=params(3),
        name="forward",
    )(weight, gates, keep, state)


def backward_kernel(
    weight_ref, factors, head_ref, grads, carry_hidden, carry_cell, sent, got, send_sems, recv_sems
):
    me, peers = actor_peers()
    meet([{"actor": peer} for peer in peers])
    carry_hidden[...] = jnp.zeros_like(carry_hidden)
    carry_cell[...] = jnp.zeros_like(carry_cell)

    def copy(t, index):
        return pltpu.make_async_remote_copy(
            src_ref=sent.at[t, index],
            dst_ref=got.at[t, index],
            send_sem=send_sems.at[t, index],
            recv_sem=recv_sems.at[t, index],
            device_id={"actor": peers[index]},
            device_id_type=MESH,
        )

    def cell_step(t):
        for chunk in range(QUARTER // 128):
            spot = pl.ds(chunk * 128, 128)
            factor = [factors[t, index, :, spot].astype(F32) for index in range(6)]
            total = head_ref[t, :, spot] + carry_hidden[:, spot]
            dcell = carry_cell[:, spot] + total * factor[0]
            carry_cell[:, spot] = dcell * factor[5]
            pieces = (dcell * factor[1], dcell * factor[2], dcell * factor[3], total * factor[4])
            for k, piece in enumerate(pieces):
                grads[t, :, pl.ds(k * QUARTER + chunk * 128, 128)] = piece.astype(BF)

    def product(t, quarter):
        return jnp.dot(
            grads[t], weight_ref[:, columns(quarter)], preferred_element_type=F32
        )

    def step(i, carry):
        t = STEPS - 1 - i
        cell_step(t)
        for index in (2, 1, 0):
            sent[t, index] = product(t, peers[index]).astype(BF)
            copy(t, index).start()
        total = product(t, me)
        for index in (0, 1, 2):
            copy(t, index).wait_recv()
            total = total + got[t, index].astype(F32)
        carry_hidden[...] = total
        for index in range(3):
            copy(t, index).wait_send()
        return carry

    lax.fori_loop(0, STEPS - 1, step, 0)
    cell_step(0)


def backward(weight_turned, factors, head_grad):
    return pl.pallas_call(
        backward_kernel,
        out_shape=jax.ShapeDtypeStruct((STEPS, BATCH, UNITS), BF),
        in_specs=[VMEM] * 3,
        out_specs=VMEM,
        scratch_shapes=[
            pltpu.VMEM((BATCH, QUARTER), F32),
            pltpu.VMEM((BATCH, QUARTER), F32),
            pltpu.VMEM((STEPS, 3, BATCH, QUARTER), BF),
            pltpu.VMEM((STEPS, 3, BATCH, QUARTER), BF),
            pltpu.SemaphoreType.DMA((STEPS, 3)),
            pltpu.SemaphoreType.DMA((STEPS, 3)),
        ],
        compiler_params=params(4),
        name="backward",
    )(weight_turned, factors, head_grad)


def flatten(values_in):
    return values_in.T.reshape(-1)


def shards(
    rec_weight,
    head_weight,
    value_head,
    gate_inputs,
    start_state,
    advantages,
    returns,
    old_logprob,
    taken_action,
    episode_start,
    segment_counts,
    assignment,
):
    learners = lax.axis_size("learn")
    place = lax.axis_index("learn")
    offset = lax.axis_index("actor") * QUARTER
    lanes = jnp.arange(learners, dtype=jnp.int32)
    own_count = jnp.sum(jnp.where(lanes == place, segment_counts, 0))
    live = (jnp.arange(BATCH, dtype=jnp.int32) < own_count).astype(F32)

    both = jnp.concatenate(
        [head_weight, value_head[:, None], jnp.zeros((64, CHOICES - 1), BF)], axis=1
    )
    heads = lax.all_gather(both, "learn", axis=0, tiled=True)

    weight = gather_weights(rec_weight.reshape(64, UNITS))
    gates = jnp.transpose(gate_inputs[0].reshape(BATCH, STEPS, UNITS), (1, 0, 2))
    keep = jnp.broadcast_to(
        (1 - episode_start[0]).astype(F32).T[:, :, None], (STEPS, BATCH, 128)
    )
    hidden, factors = forward(weight, gates, keep, start_state[0].reshape(BATCH, 2 * QUARTER))

    rows = hidden[1:].reshape(STEPS * BATCH, UNITS)
    scores = jnp.dot(rows, heads, preferred_element_type=F32)
    logits, estimate = scores[:, :CHOICES], scores[:, CHOICES]
    logsoft = jax.nn.log_softmax(logits, axis=-1)
    onehot = (
        lax.broadcasted_iota(jnp.int32, logits.shape, 1) == flatten(taken_action[0])[:, None]
    ).astype(F32)
    chosen = jnp.sum(logsoft * onehot, axis=1)
    ratio = jnp.exp(chosen - flatten(old_logprob[0]).astype(F32))
    share = jnp.broadcast_to(live[None, :] / STEPS, (STEPS, BATCH)).reshape(-1)
    grad_ratio = (-ratio * flatten(advantages[0]).astype(F32) + 0.5 * (ratio - 1.0)) * share
    grad_logits = (grad_ratio[:, None] * (onehot - jnp.exp(logsoft))).astype(BF)
    grad_estimate = ((estimate - flatten(returns[0]).astype(F32)) * share).astype(BF)
    grad_scores = jnp.concatenate(
        [grad_logits, grad_estimate[:, None], jnp.zeros((STEPS * BATCH, CHOICES - 1), BF)], axis=1
    )
    head_part = lax.dynamic_slice_in_dim(heads, offset, QUARTER, 0)
    head_grad = jnp.dot(grad_scores, head_part.T, preferred_element_type=F32).reshape(
        STEPS, BATCH, QUARTER
    )
    heads_partial = jnp.dot(rows.T, grad_scores, preferred_element_type=F32).astype(BF)
    heads_share = lax.psum_scatter(
        heads_partial, "learn", scatter_dimension=0, tiled=True
    ).astype(F32)

    assigned = assignment[0]
    slots = jnp.arange(BATCH, dtype=jnp.int32)
    earlier = (assigned[None, :] == assigned[:, None]) & (slots[None, :] < slots[:, None])
    target = assigned * 2 + jnp.sum(earlier.astype(jnp.int32), axis=1)
    values = estimate.reshape(STEPS, BATCH) * live[None, :]
    moved = jnp.sum(
        jnp.where((target[:, None] == slots[None, :])[:, :, None], values.T[:, None, :], 0.0), axis=0
    )
    learner_values = lax.all_to_all(
        moved.reshape(learners, 2, STEPS), "learn", split_axis=0, concat_axis=0, tiled=True
    ).reshape(1, BATCH, STEPS)

    grads = backward(weight.T, factors, head_grad)

    partial = jnp.dot(
        hidden[:STEPS].reshape(STEPS * BATCH, UNITS).T,
        grads.reshape(STEPS * BATCH, UNITS),
        preferred_element_type=F32,
    ).astype(BF)
    rec_share = reduce_gradient(partial).reshape(64, 4, QUARTER)
    return (rec_share, heads_share[:, :CHOICES], heads_share[:, CHOICES], learner_values)


def solution(mesh):
    placed = (
        P("learn", None, "actor"),
        P("learn", None),
        P("learn"),
        P("learn", None, None, None, "actor"),
        P("learn", None, None, "actor"),
        P("learn", None, None),
        P("learn", None, None),
        P("learn", None, None),
        P("learn", None, None),
        P("learn", None, None),
        P(),
        P("learn", None),
    )
    return jax.shard_map(
        shards,
        mesh=mesh,
        in_specs=placed,
        out_specs=(P("learn", None, "actor"), P("learn", None), P("learn"), P("learn", None, None)),
        check_vma=False,
    )
```

time: 1530 us -> 406 us (0.27)
  waiting for transfers between devices: 552 us -> 20.8 us
  blocking collectives: 429 us -> 0 us
  Pallas kernels: 0 us -> 289 us
  matrix products: 214 us -> 23.3 us
  other arithmetic: 147 us -> 7.65 us
  local copies, waits for them, and re-layouts: 121 us -> 43.3 us
  starting transfers between devices: 36.9 us -> 7.07 us
    reduce_scatter x18 -> x1, waiting for transfers between devices: 534 us -> 20.8 us  [shards(): lax.psum_scatter(heads_partial, 'learn', scatter_dimension=0, tiled=True)]
    pallas_call x0 -> x4, Pallas kernels: none -> 289 us  [the longest x1 96.2 us: forward(): pl.pallas_call(forward_kernel, out_shape=(jax.ShapeDtypeStruct((STEPS + 1...]
    unnamed x2 -> x0, blocking collectives: 237 us -> none
    all_gather x18 -> x0, blocking collectives: 192 us -> none  [the longest x16 93.6 us: advance(): hidden_new = lax.all_gather(hidden_part, 'actor', axis=1, tiled=True)]
    dot_general x38 -> x4, matrix products: 214 us -> 23.3 us  [the longest x1 14.1 us: shards(): jnp.dot(hidden[:STEPS].reshape(STEPS * BATCH, UNITS).T, grads.reshape(STE...]
    dynamic_update_slice x48 -> x0, other arithmetic: 55.3 us -> none  [train(): lax.scan(advance, (hidden_start, cell_start), (inputs, keep_masks))]
    mul x32 -> x1, other arithmetic: 32.8 us -> 0.01 us  [shards(): (-ratio * flatten(advantages[0]).astype(F32) + 0.5 * (ratio - 1.0)) * share]
    all_to_all x5 -> x1, starting transfers between devices: 36 us -> 6.99 us  [shards(): lax.all_to_all(moved.reshape(learners, 2, STEPS), 'learn', split_axis=0,...]
  transfers between devices with their start and end apart: 24 -> 3, of which waited for: 21 -> 1; matrix products, arithmetic and copies ran while one was open for 6% -> 15% of each run, Pallas kernels for 0% -> 71%
where the time goes in v1:
time: 406 us; the launch traced here: 405 us
  Pallas kernels  289 us (71%)
  local copies, waits for them, and re-layouts  43.3 us (11%)
  matrix products  23.3 us (6%)
  waiting for transfers between devices  20.8 us (5%)
  between operations  14.2 us (3%)
  other arithmetic  7.65 us (2%)
  starting transfers between devices  7.07 us (2%)
    pallas_call x1, Pallas kernels, forward(): pl.pallas_call(forward_kernel, out_shape=(jax.ShapeDtypeStruct((STEPS + 1...  96.2 us
    pallas_call x1, Pallas kernels, backward(): pl.pallas_call(backward_kernel, out_shape=jax.ShapeDtypeStruct((STEPS, BA...  82.5 us
    pallas_call x1, Pallas kernels, gather_weights(): pl.pallas_call(gather_kernel, out_shape=jax.ShapeDtypeStruct((UNITS, bloc...  55.2 us
    pallas_call x1, Pallas kernels, reduce_gradient(): pl.pallas_call(reduce_kernel, out_shape=jax.ShapeDtypeStruct((64, width),...  54.8 us
    reduce_scatter x1, waiting for transfers between devices, shards(): lax.psum_scatter(heads_partial, 'learn', scatter_dimension=0, tiled=True)  20.8 us
    another operation x2, local copies, waits for them, and re-layouts, shards(): gate_inputs[0].reshape(BATCH, STEPS, UNITS)  14.3 us
    dot_general x1, matrix products, shards(): jnp.dot(hidden[:STEPS].reshape(STEPS * BATCH, UNITS).T, grads.reshape(STE...  14.1 us
    pallas_call x1, local copies, waits for them, and re-layouts, gather_weights(): pl.pallas_call(gather_kernel, out_shape=jax.ShapeDtypeStruct((UNITS, bloc...  12.3 us
  transfers between devices with their start and end apart: 3, of which 1 were waited for; matrix products, arithmetic and copies ran while one was open for 15% of the time, Pallas kernels for 71%

profile of v1, /device:TPU:0, one launch (start us, length us, event | category | flops | bytes accessed | tf_op | source)
XLA Modules:
  0.0 405.0 jit_solution(13751410619582785187)
XLA Ops:
  7.2 0.0 all-gather.2.cloned.1.call-start
  7.2 0.8 copy.27
  8.0 0.1 pad.5.clone
  8.1 1.3 maximum_maximum_fusion.3
  9.4 0.0 reduce-scatter.2.cloned.1.call-start
  9.5 1.3 fusion.5
  10.8 0.6 compare_select_fusion.1
  11.4 0.1 reshape.135
  11.5 0.1 reshape.134
  11.6 0.8 eq.44
  12.4 0.7 convert_bitcast_fusion.1
  13.0 0.1 reshape.141
  13.1 0.7 convert_bitcast_fusion
  13.8 0.1 reshape.142
  13.9 0.7 convert_bitcast_fusion.2
  14.6 0.1 reshape.140
  14.6 1.6 copy.33
  16.2 1.7 copy.32
  17.9 7.8 %reshape.147 = bf16[64,16,2048]{2,1,0:T(8,128)(2,1)} reshape(bf16[1,64,16,4,512]{4,3,2,1,0:T(4,128)(2,1)} %param.15) | data formatting | bytes 8388608 | tf_op jit(solution)/shard_map/reshape;squeeze | solution.py:584
  25.7 6.5 %copy.35 = bf16[64,16,2048]{2,0,1:T(8,128)(2,1)} copy(bf16[64,16,2048]{2,1,0:T(8,128)(2,1)} %reshape.147) | data formatting | bytes 8388608 | tf_op jit(solution)/shard_map/reshape;squeeze | solution.py:584
  32.2 55.2 %gather_weights.1.weight_ref = bf16[2048,2048]{1,0:T(8,128)(2,1)} custom-call(bf16[64,2048]{1,0:T(8,128)(2,1)} %bitcast.52), custom_call_target="tpu_custom_call" | custom-call | tf_op jit(solution)/shard_map/gather_weights/pallas_call | solution.py:194
  87.4 12.3 %copy.26 = bf16[2048,2048]{0,1:T(8,128)(2,1)} copy(bf16[2048,2048]{1,0:T(8,128)(2,1)} %gather_weights.1.weight_ref) | data formatting | bytes 16777216 | tf_op jit(solution)/shard_map/gather_weights/pallas_call | solution.py:194
  99.7 1.0 broadcast_in_dim.31.keep_ref
  100.7 96.2 %forward.1 = (bf16[17,64,2048]{2,1,0:T(8,128)(2,1)}, bf16[16,6,64,512]{3,2,1,0:T(8,128)(2,1)}) custom-call(bf16[2048,2048]{1,0:T(8,128)(2,1)} %gather_weights.1.weight_ref, bf16[16,64,2048]{2,1,0:T(8,128)(2,1)} %bitcast.48, f32[16,64,128]{2,1,0:T(8,128)} %broadcast_in_dim.31.keep_ref, bf16[64,1024]{1,0:T(8,128)(2,1)} %bitcast.53), custom_call_target="tpu_custom_call" | custom-call | tf_op jit(solution)/shard_map/forward/pallas_call | solution.py:462
  196.9 4.8 %slice.19 = bf16[16,64,2048]{2,1,0:T(8,128)(2,1)} slice(bf16[17,64,2048]{2,1,0:T(8,128)(2,1)} %get-tuple-element.6), slice={[1:17], [0:64], [0:2048]} | slice | bytes 8388608 | tf_op jit(solution)/shard_map/slice | solution.py:590
  201.7 0.6 compare_convert_fusion
  202.4 0.2 convert_reduce_fusion
  202.5 0.1 iota_compare_fusion.1
  202.7 3.9 fusion.9
  206.7 0.1 exponential_reduce_fusion
  206.8 0.1 select_reduce_fusion.1
  206.9 0.2 multiply_convert_fusion
  207.1 2.4 convolution_convert_fusion
  209.5 0.1 reshape_squeeze.11
  209.6 0.1 copy.28
  209.7 0.2 select_reduce_fusion
  209.9 0.7 copy.29
  210.6 7.0 %all-to-all-start = ((f32[32,2,16]{2,1,0:T(2,128)}), f32[32,2,16]{2,1,0:T(2,128)S(1)}, u32[]{:S(2)}, u32[]{:S(2)}) async-start(f32[32,2,16]{2,1,0:T(2,128)} %bitcast.18), calls=%async_computation.1 | async-start | bytes 65536 | tf_op jit(solution)/shard_map/all_to_all | solution.py:623
  217.6 2.9 fusion
  220.5 82.5 %backward.1 = bf16[16,64,2048]{2,1,0:T(8,128)(2,1)} custom-call(bf16[2048,2048]{1,0:T(8,128)(2,1)} %bitcast.47, bf16[16,6,64,512]{3,2,1,0:T(8,128)(2,1)} %get-tuple-element.7.factors, f32[16,64,512]{2,1,0:T(8,128)} %bitcast.49), custom_call_target="tpu_custom_call" | custom-call | tf_op jit(solution)/shard_map/backward/pallas_call | solution.py:535
  303.0 14.1 %bitcast_convert_fusion.own = bf16[2048,2048]{1,0:T(8,128)(2,1)} fusion(bf16[17,64,2048]{2,1,0:T(8,128)(2,1)} %get-tuple-element.6, bf16[16,64,2048]{2,1,0:T(8,128)(2,1)} %backward.1), kind=kOutput, calls=%fused_computation | convolution fusion | flops 8594128896 | bytes 17039360 | tf_op jit(solution)/shard_map/dot_general | solution.py:629
  317.1 54.8 %reduce_gradient.1 = f32[64,2048]{1,0:T(8,128)} custom-call(bf16[2048,2048]{1,0:T(8,128)(2,1)} %bitcast_convert_fusion.own), custom_call_target="tpu_custom_call" | custom-call | tf_op jit(solution)/shard_map/reduce_gradient/pallas_call | solution.py:330
  371.9 2.2 reshape.137
  374.0 0.7 copy.30
  374.7 20.8 %reduce-scatter.2.cloned.1.call-done = bf16[64,256]{1,0:T(8,128)(2,1)} async-done(((bf16[2048,256]{1,0:T(8,128)(2,1)}), bf16[64,256]{1,0:T(8,128)(2,1)}) %reduce-scatter.2.cloned.1.call-update) | async-done | bytes 32784 | tf_op jit(solution)/shard_map/reduce_scatter | solution.py:611
  395.5 0.8 convert_element_type.106
  396.2 0.6 slice_reduce_fusion.1
  396.9 1.3 slice.26
  (19 shorter events, 0.2 us)
Async XLA Ops:
  7.2 195.5 %all-gather.2.cloned.1.call-start = ((), (), s32[]{:S(2)}) async-start(), calls=%async_computation.2 | async-start | bytes 1081344 | tf_op jit(solution)/shard_map/all_gather | solution.py:581
  9.4 386.1 %reduce-scatter.2.cloned.1.call-start = ((), (), s32[]{:S(2)}) async-start(), calls=%async_computation.3 | async-start | bytes 1081344 | tf_op jit(solution)/shard_map/reduce_scatter | solution.py:611
  87.4 12.3 %copy-start.1 = (s32[1,64,16]{1,2,0:T(8,128)S(1)}, s32[1,64,16]{1,2,0:T(8,128)}, u32[]{:S(2)}) copy-start(s32[1,64,16]{1,2,0:T(8,128)} %param.21) | copy-start | bytes 12292
  196.9 5.4 %copy-start.2 = (s32[1,64]{1,0:T(1,128)S(1)}, s32[1,64]{1,0:T(1,128)}, u32[]{:S(2)}) copy-start(s32[1,64]{1,0:T(1,128)} %param.23) | copy-start | bytes 772
  202.7 4.4 %copy-start = (bf16[16,64,2048]{2,1,0:T(8,128)(2,1)S(1)}, bf16[16,64,2048]{2,1,0:T(8,128)(2,1)}, u32[]{:S(2)}) copy-start(bf16[16,64,2048]{2,1,0:T(8,128)(2,1)} %slice.19) | copy-start | bytes 12582916
  210.6 163.5 %all-to-all-start = ((f32[32,2,16]{2,1,0:T(2,128)}), f32[32,2,16]{2,1,0:T(2,128)S(1)}, u32[]{:S(2)}, u32[]{:S(2)}) async-start(f32[32,2,16]{2,1,0:T(2,128)} %bitcast.18), calls=%async_computation.1 | async-start | bytes 65536 | tf_op jit(solution)/shard_map/all_to_all | solution.py:623
Sparse Core Ops, SparseCore 0:
  11.5 70.7 all-gather.1
  209.6 185.8 reduce-scatter.1

commit v2 on v1

v2 whole, which is shorter than its diff:
```python
import jax
import jax.numpy as jnp
from jax import lax
from jax.experimental import pallas as pl
from jax.experimental.pallas import tpu as pltpu
from jax.sharding import PartitionSpec as P

MESH = pl.DeviceIdType.MESH
BF = jnp.bfloat16
F32 = jnp.float32
UNITS = 2048
QUARTER = 512
BATCH = 64
STEPS = 16
CHOICES = 128
WIDE = UNITS + 2 * CHOICES
VMEM = pl.BlockSpec(memory_space=pltpu.VMEM)
LIMIT = 60 * 2**20
OFFSETS = (2, -1, 1, 0)


def params(collective):
    return pltpu.CompilerParams(
        collective_id=collective, has_side_effects=True, vmem_limit_bytes=LIMIT
    )


def meet(devices):
    barrier = pltpu.get_barrier_semaphore()
    for device in devices:
        pl.semaphore_signal(barrier, inc=1, device_id=device, device_id_type=MESH)
    pl.semaphore_wait(barrier, len(devices))


class Torus:
    def __init__(self):
        place = lax.axis_index("learn")
        self.z, self.x, self.y = place // 16, lax.rem(place // 4, 4), lax.rem(place, 4)

    def device(self, dz, dx, dy):
        z = lax.rem(self.z + dz, 2)
        x = lax.rem(self.x + dx + 4, 4)
        y = lax.rem(self.y + dy + 4, 4)
        return {"learn": z * 16 + x * 4 + y}

    def first(self, half, d):
        return self.device(0, d, 0) if half == 0 else self.device(0, 0, d)

    def second(self, half, d):
        return self.device(0, 0, d) if half == 0 else self.device(0, d, 0)

    def other(self):
        return self.device(1, 0, 0)

    def neighbours(self):
        return [
            self.device(0, 1, 0),
            self.device(0, -1, 0),
            self.device(0, 0, 1),
            self.device(0, 0, -1),
            self.other(),
        ]

    def rows(self, half, plane, dp, dq, part=None):
        dx, dy = (dp, dq) if half == 0 else (dq, dp)
        block = self.device(plane, dx, dy)["learn"]
        start = block * 64 + 32 * half
        if part is None:
            return pl.ds(pl.multiple_of(start, 32), 32)
        return pl.ds(pl.multiple_of(start + 16 * part, 16), 16)


def gather_keys():
    keys = []
    for half in (0, 1):
        keys += [("p", half, d) for d in (1, -1)]
        keys += [("pf", half, d) for d in (1, -1)]
        keys += [("z", half, dp) for dp in OFFSETS]
        for plane in (0, 1):
            for dp in OFFSETS:
                keys += [("q", half, plane, dp, d) for d in (1, -1)]
                keys += [("qf", half, plane, dp, d) for d in (1, -1)]
    return {key: index for index, key in enumerate(keys)}


KEYS = gather_keys()


def gather_blocks(held, send_sems, recv_sems):
    torus = Torus()
    started = []

    def move(key, rows, device):
        index = KEYS[key]
        return pltpu.make_async_remote_copy(
            src_ref=held.at[rows],
            dst_ref=held.at[rows],
            send_sem=send_sems.at[index],
            recv_sem=recv_sems.at[index],
            device_id=device,
            device_id_type=MESH,
        )

    def send(key, rows, device):
        copy = move(key, rows, device)
        copy.start()
        started.append(copy)

    def arrive(key, rows):
        move(key, rows, torus.other()).wait_recv()

    def spread(half, plane, dp):
        for d in (1, -1):
            send(("q", half, plane, dp, d), torus.rows(half, plane, dp, 0), torus.second(half, d))

    def pass_on(half, plane, dp):
        for d in (1, -1):
            part = 0 if d == 1 else 1
            arrive(("q", half, plane, dp, d), torus.rows(half, plane, dp, -d))
            send(
                ("qf", half, plane, dp, d),
                torus.rows(half, plane, dp, -d, part),
                torus.second(half, d),
            )

    def cross(half, dp):
        send(("z", half, dp), torus.rows(half, 0, dp, 0), torus.other())

    def crossed(half, dp):
        arrive(("z", half, dp), torus.rows(half, 1, dp, 0))
        spread(half, 1, dp)

    for half in (0, 1):
        for d in (1, -1):
            send(("p", half, d), torus.rows(half, 0, 0, 0), torus.first(half, d))
    for half in (0, 1):
        cross(half, 0)
        spread(half, 0, 0)
    for half in (0, 1):
        for d in (1, -1):
            part = 0 if d == 1 else 1
            arrive(("p", half, d), torus.rows(half, 0, -d, 0))
            send(("pf", half, d), torus.rows(half, 0, -d, 0, part), torus.first(half, d))
            cross(half, -d)
    for half in (0, 1):
        for d in (1, -1):
            spread(half, 0, -d)
    for half in (0, 1):
        crossed(half, 0)
        for d in (1, -1):
            part = 0 if d == 1 else 1
            arrive(("pf", half, d), torus.rows(half, 0, -2 * d, 0, part))
        cross(half, 2)
        spread(half, 0, 2)
    for half in (0, 1):
        pass_on(half, 0, 0)
    for half in (0, 1):
        for d in (1, -1):
            crossed(half, -d)
    for half in (0, 1):
        for d in (1, -1):
            pass_on(half, 0, -d)
    for half in (0, 1):
        crossed(half, 2)
    for half in (0, 1):
        pass_on(half, 1, 0)
    for half in (0, 1):
        pass_on(half, 0, 2)
    for half in (0, 1):
        for d in (1, -1):
            pass_on(half, 1, -d)
    for half in (0, 1):
        pass_on(half, 1, 2)
    for half in (0, 1):
        for plane in (0, 1):
            for dp in OFFSETS:
                for d in (1, -1):
                    part = 0 if d == 1 else 1
                    arrive(
                        ("qf", half, plane, dp, d), torus.rows(half, plane, dp, -2 * d, part)
                    )
    for copy in started:
        copy.wait_send()


def reduce_kernel(
    hidden,
    grads,
    scores,
    out_ref,
    heads_ref,
    own,
    staged,
    quarters,
    halves,
    send_sems,
    recv_sems,
):
    torus = Torus()
    meet(torus.neighbours())
    started = []
    where = {}
    counts = {16: 0, 32: 0}
    for key in KEYS:
        size = 16 if key[0] in ("qf", "pf") else 32
        where[key] = counts[size]
        counts[size] += 1

    def landing(key):
        size = 16 if key[0] in ("qf", "pf") else 32
        buffer = quarters if size == 16 else halves
        return buffer.at[pl.ds(where[key] * size, size)]

    def send(key, source, device):
        index = KEYS[key]
        copy = pltpu.make_async_remote_copy(
            src_ref=source,
            dst_ref=landing(key),
            send_sem=send_sems.at[index],
            recv_sem=recv_sems.at[index],
            device_id=device,
            device_id_type=MESH,
        )
        copy.start()
        started.append(copy)

    def arrived(key):
        index = KEYS[key]
        ref = landing(key)
        pltpu.make_async_remote_copy(
            src_ref=ref,
            dst_ref=ref,
            send_sem=send_sems.at[index],
            recv_sem=recv_sems.at[index],
            device_id=torus.other(),
            device_id_type=MESH,
        ).wait_recv()
        return ref[...].astype(F32)

    stage = {}

    def slot(key):
        if key not in stage:
            stage[key] = len(stage)
        return staged.at[pl.ds(stage[key] * 32, 32)]

    def multiply(plane, dx):
        first = torus.device(plane, dx, 0)["learn"] // 4
        spot = pl.ds(pl.multiple_of(first * 256, 256), 256)
        kept = hidden[0:STEPS, :, spot].reshape(STEPS * BATCH, 256)
        for k in range(4):
            part = pl.ds(k * QUARTER, QUARTER)
            own[spot, part] = lax.dot_general(
                kept,
                grads[:, :, part].reshape(STEPS * BATCH, QUARTER),
                (((0,), (0,)), ((), ())),
                preferred_element_type=F32,
            ).astype(BF)
        own[spot, UNITS:WIDE] = lax.dot_general(
            hidden[1 : STEPS + 1, :, spot].reshape(STEPS * BATCH, 256),
            scores[1 : STEPS + 1].reshape(STEPS * BATCH, 2 * CHOICES),
            (((0,), (0,)), ((), ())),
            preferred_element_type=F32,
        ).astype(BF)

    def far(half, plane, dp):
        for d in (1, -1):
            part = 0 if d == 1 else 1
            send(
                ("qf", half, plane, dp, d),
                own.at[torus.rows(half, plane, dp, -2 * d, part)],
                torus.second(half, -d),
            )

    def near(half, plane, dp, d):
        part = 0 if d == 1 else 1
        target = slot(("q", half, plane, dp, d))
        target[...] = own[torus.rows(half, plane, dp, -d), :]
        extra = arrived(("qf", half, plane, dp, d))
        rows = pl.ds(16 * part, 16)
        target[rows, :] = (target[rows, :].astype(F32) + extra).astype(BF)
        send(("q", half, plane, dp, d), target, torus.second(half, -d))

    def line(half, plane, dp):
        total = own[torus.rows(half, plane, dp, 0), :].astype(F32)
        for d in (1, -1):
            total = total + arrived(("q", half, plane, dp, d))
        return total

    def cross(half, dp):
        target = slot(("z", half, dp))
        target[...] = line(half, 1, dp).astype(BF)
        send(("z", half, dp), target, torus.other())

    def plane_sum(half, dp):
        return line(half, 0, dp) + arrived(("z", half, dp))

    for plane in (1, 0):
        multiply(plane, 2)
        for dp in OFFSETS:
            far(1, plane, dp)
        far(0, plane, 2)
        multiply(plane, -1)
        far(0, plane, -1)
        for d in (1, -1):
            near(0, plane, 2, d)
        for dp in OFFSETS:
            near(1, plane, dp, 1)
        multiply(plane, 1)
        far(0, plane, 1)
        for d in (1, -1):
            near(0, plane, -1, d)
        for dp in OFFSETS:
            near(1, plane, dp, -1)
        multiply(plane, 0)
        far(0, plane, 0)
        for d in (1, -1):
            near(0, plane, 1, d)
        for d in (1, -1):
            near(0, plane, 0, d)
    for dp in OFFSETS:
        for half in (0, 1):
            cross(half, dp)
    for half in (0, 1):
        target = slot(("pf", half))
        target[...] = plane_sum(half, 2).astype(BF)
        for d in (1, -1):
            part = 0 if d == 1 else 1
            send(("pf", half, d), target.at[pl.ds(16 * part, 16)], torus.first(half, -d))
    for half in (0, 1):
        for d in (1, -1):
            part = 0 if d == 1 else 1
            target = slot(("p", half, d))
            target[...] = plane_sum(half, -d).astype(BF)
            extra = arrived(("pf", half, d))
            rows = pl.ds(16 * part, 16)
            target[rows, :] = (target[rows, :].astype(F32) + extra).astype(BF)
            send(("p", half, d), target, torus.first(half, -d))
    for half in (0, 1):
        total = plane_sum(half, 0)
        for d in (1, -1):
            total = total + arrived(("p", half, d))
        rows = pl.ds(32 * half, 32)
        for k in range(4):
            out_ref[rows, k, :] = total[:, k * QUARTER : (k + 1) * QUARTER]
        heads_ref[rows, :] = total[:, UNITS:]
    for copy in started:
        copy.wait_send()


def reduce_gradient(hidden, grads, scores):
    quarters = sum(1 for key in KEYS if key[0] in ("qf", "pf"))
    halves = len(KEYS) - quarters
    return pl.pallas_call(
        reduce_kernel,
        out_shape=(
            jax.ShapeDtypeStruct((64, 4, QUARTER), F32),
            jax.ShapeDtypeStruct((64, 2 * CHOICES), F32),
        ),
        in_specs=[VMEM] * 3,
        out_specs=(VMEM, VMEM),
        scratch_shapes=[
            pltpu.VMEM((UNITS, WIDE), BF),
            pltpu.VMEM((46 * 32, WIDE), BF),
            pltpu.VMEM((quarters * 16, WIDE), BF),
            pltpu.VMEM((halves * 32, WIDE), BF),
            pltpu.SemaphoreType.DMA((len(KEYS),)),
            pltpu.SemaphoreType.DMA((len(KEYS),)),
        ],
        compiler_params=params(2),
        name="reduce_gradient",
    )(hidden, grads, scores)


def actor_peers():
    me = lax.axis_index("actor")
    core = me + 1 - 2 * lax.rem(me, 2)
    across = lax.rem(me + 2, 4)
    return me, (core, across, 3 - me)


def columns(quarter, start=0, size=QUARTER):
    return pl.ds(pl.multiple_of(quarter * QUARTER + start, min(size, 256)), size)


def sigmoid(value):
    return 0.5 * jnp.tanh(0.5 * value) + 0.5


HALF = QUARTER // 2


def train_kernel(
    block_ref,
    head_ref,
    gate_ref,
    state_ref,
    aux_ref,
    hidden,
    grads,
    scores,
    values,
    held,
    turned,
    factors,
    head_grad,
    gates,
    aux,
    preact,
    cell,
    carry_hidden,
    carry_cell,
    sent,
    got,
    sent_core,
    got_core,
    gather_send,
    gather_recv,
    step_send,
    step_recv,
    back_send,
    back_recv,
):
    torus = Torus()
    me, peers = actor_peers()
    core, across, diagonal = peers
    meet(torus.neighbours() + [{"actor": peer} for peer in peers])
    place = lax.axis_index("learn")
    mine = pl.ds(pl.multiple_of(place * 64, 64), 64)
    held[mine, 0:UNITS] = block_ref[...].reshape(64, UNITS)
    held[mine, UNITS:WIDE] = head_ref[...]

    def pieces(t):
        return (
            (hidden.at[t, :, columns(me)], core),
            (hidden.at[t, :, columns(me, 0, HALF)], across),
            (hidden.at[t, :, columns(me, HALF, HALF)], across),
            (hidden.at[t, :, columns(me, HALF, HALF)], diagonal),
            (hidden.at[t, :, columns(across, 0, HALF)], core),
        )

    def landed(t):
        return (
            hidden.at[t, :, columns(core)],
            hidden.at[t, :, columns(across, 0, HALF)],
            hidden.at[t, :, columns(across, HALF, HALF)],
            hidden.at[t, :, columns(diagonal, HALF, HALF)],
            hidden.at[t, :, columns(diagonal, 0, HALF)],
        )

    def step_copy(t, index):
        part, peer = pieces(t)[index]
        return pltpu.make_async_remote_copy(
            src_ref=part,
            dst_ref=part,
            send_sem=step_send.at[t, index],
            recv_sem=step_recv.at[t, index],
            device_id={"actor": peer},
            device_id_type=MESH,
        )

    def arrive(t, index):
        part = landed(t)[index]
        pltpu.make_async_remote_copy(
            src_ref=part,
            dst_ref=part,
            send_sem=step_send.at[t, index],
            recv_sem=step_recv.at[t, index],
            device_id={"actor": core},
            device_id_type=MESH,
        ).wait_recv()

    def multiply(t, spot, first=False):
        part = hidden[t, :, spot]
        for k in range(4):
            wide = pl.ds(k * QUARTER, QUARTER)
            product = jnp.dot(part, held[spot, wide], preferred_element_type=F32)
            if first:
                preact[:, wide] = product
            else:
                preact[:, wide] += product

    def column(t, kind):
        lane = lax.broadcasted_iota(jnp.int32, (BATCH, 128), 1)
        return jnp.sum(jnp.where(lane == t + 16 * kind, aux[...], 0.0), axis=1, keepdims=True)

    def heads(index):
        t = index - 1
        result = jnp.dot(hidden[index], held[:, UNITS:WIDE], preferred_element_type=F32)
        logits = result[:, 0:CHOICES]
        estimate = result[:, CHOICES : CHOICES + 1]
        share = aux[:, 80:81]
        lane = lax.broadcasted_iota(jnp.int32, (BATCH, CHOICES), 1)
        onehot = (lane.astype(F32) == column(t, 4)).astype(F32)
        shifted = logits - jnp.max(logits, axis=1, keepdims=True)
        powers = jnp.exp(shifted)
        total = jnp.sum(powers, axis=1, keepdims=True)
        chosen = jnp.sum(shifted * onehot, axis=1, keepdims=True) - jnp.log(total)
        ratio = jnp.exp(chosen - column(t, 3))
        slope = (0.5 * (ratio - 1.0) - ratio * column(t, 1)) * share
        grad_logits = slope * (onehot - powers / total)
        grad_estimate = (estimate - column(t, 2)) * share
        scores[index, :, 0:CHOICES] = grad_logits.astype(BF)
        scores[index, :, CHOICES : 2 * CHOICES] = jnp.where(lane == 0, grad_estimate, 0.0).astype(BF)
        live = (share > 0.0).astype(F32)
        values[...] = jnp.where(lane == t, estimate * live, values[...])
        head_grad[index] = lax.dot_general(
            scores[index],
            held[columns(me), UNITS:WIDE],
            (((1,), (1,)), ((), ())),
            preferred_element_type=F32,
        )

    def cells(t, half):
        keep = column(t, 0)
        for chunk in range(2 * half, 2 * half + 2):
            spot = pl.ds(chunk * 128, 128)
            kept = keep * cell[:, spot]
            inputs = []
            for k in range(4):
                wide = pl.ds(k * QUARTER + chunk * 128, 128)
                inputs.append(gates[:, wide].astype(F32) + keep * preact[:, wide])
            inp = sigmoid(inputs[0])
            forget = sigmoid(inputs[1])
            cand = jnp.tanh(inputs[2])
            outg = sigmoid(inputs[3])
            new_cell = forget * kept + inp * cand
            squash = jnp.tanh(new_cell)
            cell[:, spot] = new_cell
            part = pl.ds(pl.multiple_of(me * QUARTER + chunk * 128, 128), 128)
            hidden[t + 1, :, part] = (outg * squash).astype(BF)
            kept_factors = (
                outg * (1.0 - squash * squash),
                keep * cand * inp * (1.0 - inp),
                kept * forget * (1.0 - forget),
                keep * inp * (1.0 - cand * cand),
                keep * squash * outg * (1.0 - outg),
                keep * forget,
            )
            for index, value in enumerate(kept_factors):
                factors[t, index, :, spot] = value.astype(BF)

    hidden[0, :, columns(me)] = state_ref[:, 0, :]
    for index in (1, 2, 3, 0):
        step_copy(0, index).start()
    cell[...] = state_ref[:, 1, :].astype(F32)
    aux[...] = aux_ref[...].T[0:BATCH]
    values[...] = jnp.zeros_like(values)
    gather_blocks(held, gather_send, gather_recv)

    def step(t, carry):
        multiply(t, columns(me), True)
        gates[...] = gate_ref[:, t].reshape(BATCH, UNITS)
        arrive(t, 0)
        multiply(t, columns(core))
        stripe = pl.ds(pl.multiple_of(t * 128, 128), 128)
        turned[:, stripe] = held[stripe, 0:UNITS].T
        arrive(t, 1)
        step_copy(t, 4).start()
        multiply(t, columns(across, 0, HALF))

        @pl.when(t >= 2)
        def _():
            heads(t - 1)

        arrive(t, 2)
        multiply(t, columns(across, HALF, HALF))
        arrive(t, 3)
        multiply(t, columns(diagonal, HALF, HALF))
        arrive(t, 4)
        multiply(t, columns(diagonal, 0, HALF))
        cells(t, 0)
        step_copy(t + 1, 1).start()
        cells(t, 1)
        for index in (2, 3, 0):
            step_copy(t + 1, index).start()
        for index in range(5):
            step_copy(t, index).wait_send()
        return carry

    lax.fori_loop(0, STEPS, step, 0)
    heads(STEPS - 1)
    arrive(STEPS, 1)
    step_copy(STEPS, 4).start()
    for index in (0, 2, 3, 4):
        arrive(STEPS, index)
    for index in range(5):
        step_copy(STEPS, index).wait_send()
    heads(STEPS)

    carry_hidden[...] = jnp.zeros_like(carry_hidden)
    carry_cell[...] = jnp.zeros_like(carry_cell)

    targets = (diagonal, across, core, across, core)

    def back_copy(t, index):
        return pltpu.make_async_remote_copy(
            src_ref=sent_core.at[t] if index == 4 else sent.at[t, index],
            dst_ref=got_core.at[t] if index == 4 else got.at[t, index],
            send_sem=back_send.at[t, index],
            recv_sem=back_recv.at[t, index],
            device_id={"actor": targets[index]},
            device_id_type=MESH,
        )

    def cell_back(t):
        for chunk in range(QUARTER // 128):
            spot = pl.ds(chunk * 128, 128)
            factor = [factors[t, index, :, spot].astype(F32) for index in range(6)]
            total = head_grad[t + 1, :, spot] + carry_hidden[:, spot]
            dcell = carry_cell[:, spot] + total * factor[0]
            carry_cell[:, spot] = dcell * factor[5]
            parts = (dcell * factor[1], dcell * factor[2], dcell * factor[3], total * factor[4])
            for k, part in enumerate(parts):
                grads[t, :, pl.ds(k * QUARTER + chunk * 128, 128)] = part.astype(BF)

    def product(t, spot):
        return jnp.dot(grads[t], turned[:, spot], preferred_element_type=F32)

    def back(i, carry):
        t = STEPS - 1 - i
        cell_back(t)
        for index, quarter, start in ((0, diagonal, 0), (1, across, 0), (2, diagonal, HALF)):
            sent[t, index] = product(t, columns(quarter, start, HALF)).astype(BF)
            back_copy(t, index).start()
        part = product(t, columns(across, HALF, HALF))
        sent_core[t] = product(t, columns(core)).astype(BF)
        back_copy(t, 4).start()
        back_copy(t, 2).wait_recv()
        sent[t, 3] = (part + got[t, 2].astype(F32)).astype(BF)
        back_copy(t, 3).start()
        carry_hidden[...] = product(t, columns(me))
        back_copy(t, 4).wait_recv()
        carry_hidden[...] += got_core[t].astype(F32)
        for index in (0, 1):
            back_copy(t, index).wait_recv()
        carry_hidden[:, 0:HALF] += got[t, 0].astype(F32) + got[t, 1].astype(F32)
        back_copy(t, 3).wait_recv()
        carry_hidden[:, HALF:QUARTER] += got[t, 3].astype(F32)
        for index in range(5):
            back_copy(t, index).wait_send()
        return carry

    lax.fori_loop(0, STEPS - 1, back, 0)
    cell_back(0)


def train(block, heads, gates, state, aux):
    return pl.pallas_call(
        train_kernel,
        out_shape=(
            jax.ShapeDtypeStruct((STEPS + 1, BATCH, UNITS), BF),
            jax.ShapeDtypeStruct((STEPS, BATCH, UNITS), BF),
            jax.ShapeDtypeStruct((STEPS + 1, BATCH, 2 * CHOICES), BF),
            jax.ShapeDtypeStruct((BATCH, 128), F32),
        ),
        in_specs=[VMEM] * 5,
        out_specs=(VMEM,) * 4,
        scratch_shapes=[
            pltpu.VMEM((UNITS, WIDE), BF),
            pltpu.VMEM((UNITS, UNITS), BF),
            pltpu.VMEM((STEPS, 6, BATCH, QUARTER), BF),
            pltpu.VMEM((STEPS + 1, BATCH, QUARTER), F32),
            pltpu.VMEM((BATCH, UNITS), BF),
            pltpu.VMEM((BATCH, 128), F32),
            pltpu.VMEM((BATCH, UNITS), F32),
            pltpu.VMEM((BATCH, QUARTER), F32),
            pltpu.VMEM((BATCH, QUARTER), F32),
            pltpu.VMEM((BATCH, QUARTER), F32),
            pltpu.VMEM((STEPS, 4, BATCH, HALF), BF),
            pltpu.VMEM((STEPS, 4, BATCH, HALF), BF),
            pltpu.VMEM((STEPS, BATCH, QUARTER), BF),
            pltpu.VMEM((STEPS, BATCH, QUARTER), BF),
            pltpu.SemaphoreType.DMA((len(KEYS),)),
            pltpu.SemaphoreType.DMA((len(KEYS),)),
            pltpu.SemaphoreType.DMA((STEPS + 1, 5)),
            pltpu.SemaphoreType.DMA((STEPS + 1, 5)),
            pltpu.SemaphoreType.DMA((STEPS, 5)),
            pltpu.SemaphoreType.DMA((STEPS, 5)),
        ],
        compiler_params=params(1),
        name="train",
    )(block, heads, gates, state, aux)


def shards(
    rec_weight,
    head_weight,
    value_head,
    gate_inputs,
    start_state,
    advantages,
    returns,
    old_logprob,
    taken_action,
    episode_start,
    segment_counts,
    assignment,
):
    learners = lax.axis_size("learn")
    place = lax.axis_index("learn")
    lanes = jnp.arange(learners, dtype=jnp.int32)
    own_count = jnp.sum(jnp.where(lanes == place, segment_counts, 0))
    live = (jnp.arange(BATCH, dtype=jnp.int32) < own_count).astype(F32)

    heads = jnp.concatenate(
        [head_weight, value_head[:, None], jnp.zeros((64, CHOICES - 1), BF)], axis=1
    )
    aux = jnp.concatenate(
        [
            (1 - episode_start[0]).astype(F32).T,
            advantages[0].astype(F32).T,
            returns[0].astype(F32).T,
            old_logprob[0].astype(F32).T,
            taken_action[0].astype(F32).T,
            jnp.broadcast_to(live[None, :] / STEPS, (48, BATCH)),
        ],
        axis=0,
    )
    aux = jnp.pad(aux, ((0, 0), (0, 128 - BATCH)))
    hidden, grads, scores, estimates = train(
        rec_weight, heads, gate_inputs[0], start_state[0], aux
    )

    assigned = assignment[0]
    slots = jnp.arange(BATCH, dtype=jnp.int32)
    earlier = (assigned[None, :] == assigned[:, None]) & (slots[None, :] < slots[:, None])
    target = assigned * 2 + jnp.sum(earlier.astype(jnp.int32), axis=1)
    moved = jnp.sum(
        jnp.where(
            (target[:, None] == slots[None, :])[:, :, None], estimates[:, None, :STEPS], 0.0
        ),
        axis=0,
    )
    learner_values = lax.all_to_all(
        moved.reshape(learners, 2, STEPS), "learn", split_axis=0, concat_axis=0, tiled=True
    ).reshape(1, BATCH, STEPS)
    rec_share, heads_share = reduce_gradient(hidden, grads, scores)
    return (rec_share, heads_share[:, :CHOICES], heads_share[:, CHOICES], learner_values)


def solution(mesh):
    placed = (
        P("learn", None, "actor"),
        P("learn", None),
        P("learn"),
        P("learn", None, None, None, "actor"),
        P("learn", None, None, "actor"),
        P("learn", None, None),
        P("learn", None, None),
        P("learn", None, None),
        P("learn", None, None),
        P("learn", None, None),
        P(),
        P("learn", None),
    )
    return jax.shard_map(
        shards,
        mesh=mesh,
        in_specs=placed,
        out_specs=(P("learn", None, "actor"), P("learn", None), P("learn"), P("learn", None, None)),
        check_vma=False,
    )
```

time: 406 us -> 323 us (0.80)
  local copies, waits for them, and re-layouts: 43.3 us -> 7.48 us
  matrix products: 23.3 us -> 0 us
  waiting for transfers between devices: 20.8 us -> 0.01 us
  between operations: 14.2 us -> 0.69 us
  Pallas kernels: 289 us -> 298 us
    dot_general x4 -> x0, matrix products: 23.3 us -> none  [the longest x1 14.1 us: shards(): jnp.dot(hidden[:STEPS].reshape(STEPS * BATCH, UNITS).T, grads.reshape(STE...]
    reduce_scatter x1 -> x0, waiting for transfers between devices: 20.8 us -> none  [shards(): lax.psum_scatter(heads_partial, 'learn', scatter_dimension=0, tiled=True)]
    another operation x3 -> x0, local copies, waits for them, and re-layouts: 14.4 us -> none  [the longest x2 14.3 us: shards(): gate_inputs[0].reshape(BATCH, STEPS, UNITS)]
    pallas_call x1 -> x0, local copies, waits for them, and re-layouts: 12.3 us -> none  [gather_weights(): pl.pallas_call(gather_kernel, out_shape=jax.ShapeDtypeStruct((UNITS, bloc...]
    pallas_call x4 -> x2, Pallas kernels: 289 us -> 298 us  [the longest x1 224 us: train(): pl.pallas_call(train_kernel, out_shape=(jax.ShapeDtypeStruct((STEPS + 1,...]
    slice x1 -> x0, local copies, waits for them, and re-layouts: 4.76 us -> none  [shards(): rows = hidden[1:].reshape(STEPS * BATCH, UNITS)]
  transfers between devices with their start and end apart: 3 -> 1, of which waited for: 1 -> 0; matrix products, arithmetic and copies ran while one was open for 15% -> 1% of each run, Pallas kernels for 71% -> 23%
where the time goes in v2:
time: 323 us
  Pallas kernels  298 us (92%)
  other arithmetic  9.36 us (3%)
  starting transfers between devices  7.58 us (2%)
  local copies, waits for them, and re-layouts  7.48 us (2%)
    pallas_call x1, Pallas kernels, train(): pl.pallas_call(train_kernel, out_shape=(jax.ShapeDtypeStruct((STEPS + 1,...  224 us
    pallas_call x1, Pallas kernels, reduce_gradient(): pl.pallas_call(reduce_kernel, out_shape=(jax.ShapeDtypeStruct((64, 4, QUA...  73.9 us
    all_to_all x1, starting transfers between devices, shards(): lax.all_to_all(moved.reshape(learners, 2, STEPS), 'learn', split_axis=0,...  7.58 us
  transfers between devices with their start and end apart: 1, of which 0 were waited for; matrix products, arithmetic and copies ran while one was open for 1% of the time, Pallas kernels for 23%

profile of v2, /device:TPU:0, one launch (start us, length us, event | category | flops | bytes accessed | tf_op | source)
XLA Modules:
  0.0 322.6 jit_solution(6133982901901996556)
XLA Ops:
  0.6 1.3 fusion.1
  1.9 0.6 compare_select_fusion
  2.6 0.9 convert_reduce_fusion
  3.5 0.7 multiply_add_fusion
  4.2 0.1 iota_compare_fusion
  4.2 0.8 copy.19
  5.0 0.7 constant_dynamic-update-slice_fusion.5
  5.7 0.1 pad.7.clone
  5.8 0.7 constant_dynamic-update-slice_fusion.4
  6.5 0.7 constant_dynamic-update-slice_fusion.3
  7.2 0.7 constant_dynamic-update-slice_fusion.2
  7.9 0.7 constant_dynamic-update-slice_fusion.1
  8.6 0.6 pad.4.aux_ref
  9.2 1.3 maximum_maximum_fusion.head_ref
  10.5 223.6 %train.1 = (bf16[17,64,2048]{2,1,0:T(8,128)(2,1)}, bf16[16,64,2048]{2,1,0:T(8,128)(2,1)}, bf16[17,64,256]{2,1,0:T(8,128)(2,1)}, f32[64,128]{1,0:T(8,128)}) custom-call(bf16[64,4,512]{2,1,0:T(4,128)(2,1)} %block_ref.1, bf16[64,256]{1,0:T(8,128)(2,1)} %maximum_maximum_fusion.head_ref, bf16[64,16,4,512]{3,2,1,0:T(4,128)(2,1)} %bitcast.37, ...), custom_call_target="tpu_custom_call" | custom-call | tf_op jit(solution)/shard_map/train/pallas_call | solution.py:649
  234.1 1.0 select_reduce_fusion
  235.1 0.7 copy.20
  235.8 7.6 %all-to-all-start = ((f32[32,2,16]{2,1,0:T(2,128)}), f32[32,2,16]{2,1,0:T(2,128)S(1)}, u32[]{:S(2)}, u32[]{:S(2)}) async-start(f32[32,2,16]{2,1,0:T(2,128)} %bitcast.14), calls=%async_computation | async-start | bytes 65536 | tf_op jit(solution)/shard_map/all_to_all | solution.py:735
  243.4 73.9 %reduce_gradient.1 = (f32[64,4,512]{2,1,0:T(4,128)}, f32[64,256]{1,0:T(8,128)}) custom-call(bf16[17,64,2048]{2,1,0:T(8,128)(2,1)} %get-tuple-element.10.hidden, bf16[16,64,2048]{2,1,0:T(8,128)(2,1)} %get-tuple-element.11.grads, bf16[17,64,256]{2,1,0:T(8,128)(2,1)} %get-tuple-element.12.scores), custom_call_target="tpu_custom_call" | custom-call | tf_op jit(solution)/shard_map/reduce_gradient/pallas_call | solution.py:354
  317.3 1.4 slice_reduce_fusion
  318.7 1.4 slice.9
  320.1 0.0 all-to-all-done
  320.1 0.7 copy.21
  320.8 1.9 copy.28
  (2 shorter events, 0.0 us)
Async XLA Ops:
  235.8 84.3 %all-to-all-start = ((f32[32,2,16]{2,1,0:T(2,128)}), f32[32,2,16]{2,1,0:T(2,128)S(1)}, u32[]{:S(2)}, u32[]{:S(2)}) async-start(f32[32,2,16]{2,1,0:T(2,128)} %bitcast.14), calls=%async_computation | async-start | bytes 65536 | tf_op jit(solution)/shard_map/all_to_all | solution.py:735

commit v3 on v2

--- a/solution.py
+++ b/solution.py
@@ -86,7 +86,7 @@
 KEYS = gather_keys()
 
 
-def gather_blocks(held, send_sems, recv_sems):
+def gather_blocks(held, send_sems, recv_sems, work):
     torus = Torus()
     started = []
 
@@ -109,6 +109,8 @@
     def arrive(key, rows):
         move(key, rows, torus.other()).wait_recv()
 
+    left = list(range(STEPS))
+
     def spread(half, plane, dp):
         for d in (1, -1):
             send(("q", half, plane, dp, d), torus.rows(half, plane, dp, 0), torus.second(half, d))
@@ -127,6 +129,9 @@
         send(("z", half, dp), torus.rows(half, 0, dp, 0), torus.other())
 
     def crossed(half, dp):
+        for t in left[:2]:
+            work(t)
+        del left[:2]
         arrive(("z", half, dp), torus.rows(half, 1, dp, 0))
         spread(half, 1, dp)
 
@@ -183,21 +188,95 @@
         copy.wait_send()
 
 
+def exchange_values(torus, assigned_ref, estimate_ref, moved, send_sems, recv_sems):
+    lane = lax.broadcasted_iota(jnp.int32, (STEPS, 128), 1)
+    phases = (
+        (0, torus.y, 2, 4, lambda d: torus.device(0, 0, d)),
+        (4, torus.x, 8, 4, lambda d: torus.device(0, d, 0)),
+        (8, torus.z, 32, 2, lambda d: torus.device(d, 0, 0)),
+    )
+
+    def copies(phase):
+        first, _, _, size, device = phases[phase]
+        return [
+            pltpu.make_async_remote_copy(
+                src_ref=moved.at[first],
+                dst_ref=moved.at[first + d],
+                send_sem=send_sems.at[first + d],
+                recv_sem=recv_sems.at[first + d],
+                device_id=device(d),
+                device_id_type=MESH,
+            )
+            for d in range(1, size)
+        ]
+
+    def start(phase):
+        for copy in copies(phase):
+            copy.start()
+
+    def finish(phase):
+        first, place, stride, size, _ = phases[phase]
+        for copy in copies(phase):
+            copy.wait()
+        field = lax.rem(lane // stride, size)
+        result = jnp.zeros((STEPS, 128), F32)
+        for d in range(size):
+            source = lax.rem(place - d + size, size)
+            shift = lax.rem((source - place) * stride + 128, 128)
+            turned = pltpu.roll(moved[first + d], shift, 1)
+            result = jnp.where(field == source, turned, result)
+        return result
+
+    def run(stage):
+        if stage == 0:
+            row = jnp.broadcast_to(assigned_ref[...].astype(F32), (BATCH, BATCH))
+            row = jnp.concatenate([row, jnp.full((BATCH, 128 - BATCH), -1.0, F32)], axis=1)
+            tall = jnp.concatenate([row, row], axis=0).T
+            column = tall[0:BATCH, :]
+            across = lax.broadcasted_iota(jnp.int32, (BATCH, 128), 1)
+            down = lax.broadcasted_iota(jnp.int32, (BATCH, 128), 0)
+            earlier = jnp.where((row == column) & (across < down), 1.0, 0.0)
+            target = 2.0 * column + jnp.sum(earlier, axis=1, keepdims=True)
+            spread = jnp.where(across.astype(F32) == target, 1.0, 0.0)
+            moved[0] = jnp.dot(
+                estimate_ref[...],
+                spread,
+                preferred_element_type=F32,
+                precision=lax.Precision.HIGHEST,
+            )
+            start(0)
+        elif stage < 3:
+            moved[phases[stage][0]] = finish(stage - 1)
+            start(stage)
+        else:
+            moved[6] = finish(2)
+
+    return run
+
+
 def reduce_kernel(
     hidden,
     grads,
     scores,
+    assigned_ref,
+    estimate_ref,
     out_ref,
-    heads_ref,
+    policy_ref,
+    value_ref,
+    values_ref,
+    value_column,
+    moved,
     own,
     staged,
     quarters,
     halves,
     send_sems,
     recv_sems,
+    value_send,
+    value_recv,
 ):
     torus = Torus()
-    meet(torus.neighbours())
+    meet(torus.neighbours() + [torus.device(0, 2, 0), torus.device(0, 0, 2)])
     started = []
     where = {}
     counts = {16: 0, 32: 0}
@@ -295,32 +374,32 @@
     def plane_sum(half, dp):
         return line(half, 0, dp) + arrived(("z", half, dp))
 
+    exchange = exchange_values(torus, assigned_ref, estimate_ref, moved, value_send, value_recv)
     for plane in (1, 0):
         multiply(plane, 2)
         for dp in OFFSETS:
             far(1, plane, dp)
         far(0, plane, 2)
-        multiply(plane, -1)
-        far(0, plane, -1)
-        for d in (1, -1):
-            near(0, plane, 2, d)
-        for dp in OFFSETS:
-            near(1, plane, dp, 1)
-        multiply(plane, 1)
-        far(0, plane, 1)
-        for d in (1, -1):
-            near(0, plane, -1, d)
-        for dp in OFFSETS:
-            near(1, plane, dp, -1)
-        multiply(plane, 0)
-        far(0, plane, 0)
-        for d in (1, -1):
-            near(0, plane, 1, d)
-        for d in (1, -1):
-            near(0, plane, 0, d)
+        for dp in (-1, 1, 0):
+            multiply(plane, dp)
+            far(0, plane, dp)
+            if plane == 1 and dp == -1:
+                exchange(0)
+        if plane == 1:
+            for dp in OFFSETS:
+                for half in (0, 1):
+                    for d in (1, -1):
+                        near(half, 1, dp, d)
+            exchange(1)
     for dp in OFFSETS:
         for half in (0, 1):
             cross(half, dp)
+    exchange(2)
+    for dp in OFFSETS:
+        for half in (0, 1):
+            for d in (1, -1):
+                near(half, 0, dp, d)
+    exchange(3)
     for half in (0, 1):
         target = slot(("pf", half))
         target[...] = plane_sum(half, 2).astype(BF)
@@ -343,33 +422,42 @@
         rows = pl.ds(32 * half, 32)
         for k in range(4):
             out_ref[rows, k, :] = total[:, k * QUARTER : (k + 1) * QUARTER]
-        heads_ref[rows, :] = total[:, UNITS:]
+        policy_ref[rows, :] = total[:, UNITS : UNITS + CHOICES]
+        value_column[rows, :] = total[:, UNITS + CHOICES :]
+    value_ref[...] = value_column[...].T[0:1, 0:64]
+    values_ref[...] = moved[6, :, 0:BATCH]
     for copy in started:
         copy.wait_send()
 
 
-def reduce_gradient(hidden, grads, scores):
+def reduce_gradient(hidden, grads, scores, assigned, estimates):
     quarters = sum(1 for key in KEYS if key[0] in ("qf", "pf"))
     halves = len(KEYS) - quarters
     return pl.pallas_call(
         reduce_kernel,
         out_shape=(
             jax.ShapeDtypeStruct((64, 4, QUARTER), F32),
-            jax.ShapeDtypeStruct((64, 2 * CHOICES), F32),
+            jax.ShapeDtypeStruct((64, CHOICES), F32),
+            jax.ShapeDtypeStruct((1, 64), F32),
+            jax.ShapeDtypeStruct((STEPS, BATCH), F32),
         ),
-        in_specs=[VMEM] * 3,
-        out_specs=(VMEM, VMEM),
+        in_specs=[VMEM] * 5,
+        out_specs=(VMEM,) * 4,
         scratch_shapes=[
+            pltpu.VMEM((64, 128), F32),
+            pltpu.VMEM((10, STEPS, 128), F32),
             pltpu.VMEM((UNITS, WIDE), BF),
             pltpu.VMEM((46 * 32, WIDE), BF),
             pltpu.VMEM((quarters * 16, WIDE), BF),
             pltpu.VMEM((halves * 32, WIDE), BF),
             pltpu.SemaphoreType.DMA((len(KEYS),)),
             pltpu.SemaphoreType.DMA((len(KEYS),)),
+            pltpu.SemaphoreType.DMA((10,)),
+            pltpu.SemaphoreType.DMA((10,)),
         ],
         compiler_params=params(2),
         name="reduce_gradient",
-    )(hidden, grads, scores)
+    )(hidden, grads, scores, assigned, estimates)
 
 
 def actor_peers():
@@ -393,12 +481,19 @@
 def train_kernel(
     block_ref,
     head_ref,
+    value_ref,
     gate_ref,
     state_ref,
-    aux_ref,
+    counts_ref,
+    start_ref,
+    advantage_ref,
+    return_ref,
+    logprob_ref,
+    action_ref,
     hidden,
     grads,
     scores,
+    estimates,
     values,
     held,
     turned,
@@ -428,7 +523,9 @@
     place = lax.axis_index("learn")
     mine = pl.ds(pl.multiple_of(place * 64, 64), 64)
     held[mine, 0:UNITS] = block_ref[...].reshape(64, UNITS)
-    held[mine, UNITS:WIDE] = head_ref[...]
+    held[mine, UNITS : UNITS + CHOICES] = head_ref[...]
+    line = jnp.concatenate([value_ref[...].astype(F32), jnp.zeros((1, 64), F32)], axis=1)
+    held[mine, UNITS + CHOICES : WIDE] = jnp.broadcast_to(line, (128, 128)).T[0:64].astype(BF)
 
     def pieces(t):
         return (
@@ -519,7 +616,7 @@
             inputs = []
             for k in range(4):
                 wide = pl.ds(k * QUARTER + chunk * 128, 128)
-                inputs.append(gates[:, wide].astype(F32) + keep * preact[:, wide])
+                inputs.append(gates[t, :, wide].astype(F32) + keep * preact[:, wide])
             inp = sigmoid(inputs[0])
             forget = sigmoid(inputs[1])
             cand = jnp.tanh(inputs[2])
@@ -544,25 +641,43 @@
     for index in (1, 2, 3, 0):
         step_copy(0, index).start()
     cell[...] = state_ref[:, 1, :].astype(F32)
-    aux[...] = aux_ref[...].T[0:BATCH]
     values[...] = jnp.zeros_like(values)
-    gather_blocks(held, gather_send, gather_recv)
+    row = lax.broadcasted_iota(jnp.int32, (BATCH, 128), 0)
+    live = jnp.where(row < counts_ref[place], 1.0 / STEPS, 0.0)
+    table = jnp.concatenate(
+        [
+            1.0 - start_ref[...].astype(F32),
+            advantage_ref[...].astype(F32),
+            return_ref[...].astype(F32),
+            logprob_ref[...].astype(F32),
+            action_ref[...].astype(F32),
+            jnp.zeros((48, BATCH), F32),
+        ],
+        axis=0,
+    )
+    table = jnp.concatenate([table, jnp.zeros((128, 128 - BATCH), F32)], axis=1)
+    lane = lax.broadcasted_iota(jnp.int32, (BATCH, 128), 1)
+    aux[...] = jnp.where(lane < 80, table.T[0:BATCH], live)
+
+    def unpack(t):
+        gates[t] = gate_ref[:, t].reshape(BATCH, UNITS)
+
+    gather_blocks(held, gather_send, gather_recv, unpack)
 
     def step(t, carry):
         multiply(t, columns(me), True)
-        gates[...] = gate_ref[:, t].reshape(BATCH, UNITS)
+        stripe = pl.ds(pl.multiple_of(t * 128, 128), 128)
+        turned[:, stripe] = held[stripe, 0:UNITS].T
         arrive(t, 0)
         multiply(t, columns(core))
-        stripe = pl.ds(pl.multiple_of(t * 128, 128), 128)
-        turned[:, stripe] = held[stripe, 0:UNITS].T
+
+        @pl.when(t >= 2)
+        def _():
+            heads(t - 1)
+
         arrive(t, 1)
         step_copy(t, 4).start()
         multiply(t, columns(across, 0, HALF))
-
-        @pl.when(t >= 2)
-        def _():
-            heads(t - 1)
-
         arrive(t, 2)
         multiply(t, columns(across, HALF, HALF))
         arrive(t, 3)
@@ -587,6 +702,7 @@
     for index in range(5):
         step_copy(STEPS, index).wait_send()
     heads(STEPS)
+    estimates[...] = jnp.concatenate([values[...], values[...]], axis=0).T[0:STEPS, 0:BATCH]
 
     carry_hidden[...] = jnp.zeros_like(carry_hidden)
     carry_cell[...] = jnp.zeros_like(carry_cell)
@@ -620,7 +736,7 @@
     def back(i, carry):
         t = STEPS - 1 - i
         cell_back(t)
-        for index, quarter, start in ((0, diagonal, 0), (1, across, 0), (2, diagonal, HALF)):
+        for index, quarter, start in ((2, diagonal, HALF), (0, diagonal, 0), (1, across, 0)):
             sent[t, index] = product(t, columns(quarter, start, HALF)).astype(BF)
             back_copy(t, index).start()
         part = product(t, columns(across, HALF, HALF))
@@ -645,23 +761,26 @@
     cell_back(0)
 
 
-def train(block, heads, gates, state, aux):
+def train(*operands):
+    specs = [VMEM] * len(operands)
+    specs[5] = pl.BlockSpec(memory_space=pltpu.SMEM)
     return pl.pallas_call(
         train_kernel,
         out_shape=(
             jax.ShapeDtypeStruct((STEPS + 1, BATCH, UNITS), BF),
             jax.ShapeDtypeStruct((STEPS, BATCH, UNITS), BF),
             jax.ShapeDtypeStruct((STEPS + 1, BATCH, 2 * CHOICES), BF),
-            jax.ShapeDtypeStruct((BATCH, 128), F32),
+            jax.ShapeDtypeStruct((STEPS, BATCH), F32),
         ),
-        in_specs=[VMEM] * 5,
+        in_specs=specs,
         out_specs=(VMEM,) * 4,
         scratch_shapes=[
+            pltpu.VMEM((BATCH, 128), F32),
             pltpu.VMEM((UNITS, WIDE), BF),
             pltpu.VMEM((UNITS, UNITS), BF),
             pltpu.VMEM((STEPS, 6, BATCH, QUARTER), BF),
             pltpu.VMEM((STEPS + 1, BATCH, QUARTER), F32),
-            pltpu.VMEM((BATCH, UNITS), BF),
+            pltpu.VMEM((STEPS, BATCH, UNITS), BF),
             pltpu.VMEM((BATCH, 128), F32),
             pltpu.VMEM((BATCH, UNITS), F32),
             pltpu.VMEM((BATCH, QUARTER), F32),
@@ -680,7 +799,7 @@
         ],
         compiler_params=params(1),
         name="train",
-    )(block, heads, gates, state, aux)
+    )(*operands)
 
 
 def shards(
@@ -697,46 +816,23 @@
     segment_counts,
     assignment,
 ):
-    learners = lax.axis_size("learn")
-    place = lax.axis_index("learn")
-    lanes = jnp.arange(learners, dtype=jnp.int32)
-    own_count = jnp.sum(jnp.where(lanes == place, segment_counts, 0))
-    live = (jnp.arange(BATCH, dtype=jnp.int32) < own_count).astype(F32)
-
-    heads = jnp.concatenate(
-        [head_weight, value_head[:, None], jnp.zeros((64, CHOICES - 1), BF)], axis=1
+    hidden, grads, scores, estimates = train(
+        rec_weight,
+        head_weight,
+        value_head[None],
+        gate_inputs[0],
+        start_state[0],
+        segment_counts,
+        episode_start[0].T,
+        advantages[0].T,
+        returns[0].T,
+        old_logprob[0].T,
+        taken_action[0].T,
     )
-    aux = jnp.concatenate(
-        [
-            (1 - episode_start[0]).astype(F32).T,
-            advantages[0].astype(F32).T,
-            returns[0].astype(F32).T,
-            old_logprob[0].astype(F32).T,
-            taken_action[0].astype(F32).T,
-            jnp.broadcast_to(live[None, :] / STEPS, (48, BATCH)),
-        ],
-        axis=0,
+    rec_share, policy_share, value_share, values = reduce_gradient(
+        hidden, grads, scores, assignment, estimates
     )
-    aux = jnp.pad(aux, ((0, 0), (0, 128 - BATCH)))
-    hidden, grads, scores, estimates = train(
-        rec_weight, heads, gate_inputs[0], start_state[0], aux
-    )
-
-    assigned = assignment[0]
-    slots = jnp.arange(BATCH, dtype=jnp.int32)
-    earlier = (assigned[None, :] == assigned[:, None]) & (slots[None, :] < slots[:, None])
-    target = assigned * 2 + jnp.sum(earlier.astype(jnp.int32), axis=1)
-    moved = jnp.sum(
-        jnp.where(
-            (target[:, None] == slots[None, :])[:, :, None], estimates[:, None, :STEPS], 0.0
-        ),
-        axis=0,
-    )
-    learner_values = lax.all_to_all(
-        moved.reshape(learners, 2, STEPS), "learn", split_axis=0, concat_axis=0, tiled=True
-    ).reshape(1, BATCH, STEPS)
-    rec_share, heads_share = reduce_gradient(hidden, grads, scores)
-    return (rec_share, heads_share[:, :CHOICES], heads_share[:, CHOICES], learner_values)
+    return (rec_share, policy_share, value_share[0], values.T[None])
 
 
 def solution(mesh):

time: 323 us -> 285 us (0.88)
  Pallas kernels: 298 us -> 278 us
  other arithmetic: 9.36 us -> 0 us
  starting transfers between devices: 7.58 us -> 0 us
    pallas_call x1, Pallas kernels: 224 us -> 214 us  [train(): pl.pallas_call(train_kernel, out_shape=(jax.ShapeDtypeStruct((STEPS + 1,...]
    pallas_call x1, Pallas kernels: 73.9 us -> 64.5 us  [reduce_gradient(): pl.pallas_call(reduce_kernel, out_shape=(jax.ShapeDtypeStruct((64, 4, QUA...]
    all_to_all x1 -> x0, starting transfers between devices: 7.58 us -> none  [shards(): lax.all_to_all(moved.reshape(learners, 2, STEPS), 'learn', split_axis=0,...]
    unnamed x5 -> x0, other arithmetic: 3.47 us -> none
  transfers between devices with their start and end apart: 1 -> 0, of which waited for: 0 -> 0; matrix products, arithmetic and copies ran while one was open for 1% -> 0% of each run, Pallas kernels for 23% -> 0%
where the time goes in v3:
time: 285 us
  Pallas kernels  278 us (98%)
  local copies, waits for them, and re-layouts  5.66 us (2%)
    pallas_call x1, Pallas kernels, train(): pl.pallas_call(train_kernel, out_shape=(jax.ShapeDtypeStruct((STEPS + 1,...  214 us
    pallas_call x1, Pallas kernels, reduce_gradient(): pl.pallas_call(reduce_kernel, out_shape=(jax.ShapeDtypeStruct((64, 4, QUA...  64.5 us

profile of v3, /device:TPU:0, one launch (start us, length us, event | category | flops | bytes accessed | tf_op | source)
XLA Modules:
  0.0 284.8 jit_solution(9478129104957729709)
XLA Ops:
  0.6 214.0 %train.1 = (bf16[17,64,2048]{2,1,0:T(8,128)(2,1)}, bf16[16,64,2048]{2,1,0:T(8,128)(2,1)}, bf16[17,64,256]{2,1,0:T(8,128)(2,1)}, f32[16,64]{1,0:T(8,128)}) custom-call(bf16[64,4,512]{2,1,0:T(4,128)(2,1)} %block_ref.1, bf16[64,128]{1,0:T(8,128)(2,1)} %head_ref.1, bf16[1,64]{1,0:T(2,128)(2,1)} %bitcast.30, bf16[64,16,4,512]{3,2,1,0:T(4,128)(2,1)} %bitcast.22, ...), custom_call_target="tpu_custom_call" | custom-call | tf_op jit(solution)/shard_map/train/pallas_call | solution.py:767
  214.6 64.5 %reduce_gradient.1 = (f32[64,4,512]{2,1,0:T(4,128)}, f32[64,128]{1,0:T(8,128)}, f32[1,64]{1,0:T(1,128)}, f32[16,64]{1,0:T(8,128)}) custom-call(bf16[17,64,2048]{2,1,0:T(8,128)(2,1)} %get-tuple-element.12.hidden, bf16[16,64,2048]{2,1,0:T(8,128)(2,1)} %get-tuple-element.13.grads, bf16[17,64,256]{2,1,0:T(8,128)(2,1)} %get-tuple-element.14.scores, ...), custom_call_target="tpu_custom_call" | custom-call | tf_op jit(solution)/shard_map/reduce_gradient/pallas_call | solution.py:436
  279.1 1.9 copy.20
  281.0 1.4 copy.21
  282.3 1.1 copy.22
  283.5 1.3 copy.23

commit v4 on v3

--- a/solution.py
+++ b/solution.py
@@ -188,7 +188,7 @@
         copy.wait_send()
 
 
-def exchange_values(torus, assigned_ref, estimate_ref, moved, send_sems, recv_sems):
+def exchange_values(torus, assigned_ref, estimates, moved, send_sems, recv_sems):
     lane = lax.broadcasted_iota(jnp.int32, (STEPS, 128), 1)
     phases = (
         (0, torus.y, 2, 4, lambda d: torus.device(0, 0, d)),
@@ -239,7 +239,7 @@
             target = 2.0 * column + jnp.sum(earlier, axis=1, keepdims=True)
             spread = jnp.where(across.astype(F32) == target, 1.0, 0.0)
             moved[0] = jnp.dot(
-                estimate_ref[...],
+                estimates,
                 spread,
                 preferred_element_type=F32,
                 precision=lax.Precision.HIGHEST,
@@ -254,29 +254,21 @@
     return run
 
 
-def reduce_kernel(
+def reduce_blocks(
+    torus,
     hidden,
     grads,
     scores,
-    assigned_ref,
-    estimate_ref,
+    exchange,
     out_ref,
     policy_ref,
     value_ref,
-    values_ref,
     value_column,
-    moved,
     own,
-    staged,
-    quarters,
-    halves,
+    arena,
     send_sems,
     recv_sems,
-    value_send,
-    value_recv,
 ):
-    torus = Torus()
-    meet(torus.neighbours() + [torus.device(0, 2, 0), torus.device(0, 0, 2)])
     started = []
     where = {}
     counts = {16: 0, 32: 0}
@@ -287,8 +279,8 @@
 
     def landing(key):
         size = 16 if key[0] in ("qf", "pf") else 32
-        buffer = quarters if size == 16 else halves
-        return buffer.at[pl.ds(where[key] * size, size)]
+        base = 0 if size == 32 else counts[32] * 32
+        return arena.at[pl.ds(base + where[key] * size, size)]
 
     def send(key, source, device):
         index = KEYS[key]
@@ -315,13 +307,6 @@
             device_id_type=MESH,
         ).wait_recv()
         return ref[...].astype(F32)
-
-    stage = {}
-
-    def slot(key):
-        if key not in stage:
-            stage[key] = len(stage)
-        return staged.at[pl.ds(stage[key] * 32, 32)]
 
     def multiply(plane, dx):
         first = torus.device(plane, dx, 0)["learn"] // 4
@@ -353,12 +338,11 @@
 
     def near(half, plane, dp, d):
         part = 0 if d == 1 else 1
-        target = slot(("q", half, plane, dp, d))
-        target[...] = own[torus.rows(half, plane, dp, -d), :]
         extra = arrived(("qf", half, plane, dp, d))
-        rows = pl.ds(16 * part, 16)
-        target[rows, :] = (target[rows, :].astype(F32) + extra).astype(BF)
-        send(("q", half, plane, dp, d), target, torus.second(half, -d))
+        rows = torus.rows(half, plane, dp, -d, part)
+        own[rows, :] = (own[rows, :].astype(F32) + extra).astype(BF)
+        block = own.at[torus.rows(half, plane, dp, -d)]
+        send(("q", half, plane, dp, d), block, torus.second(half, -d))
 
     def line(half, plane, dp):
         total = own[torus.rows(half, plane, dp, 0), :].astype(F32)
@@ -367,31 +351,31 @@
         return total
 
     def cross(half, dp):
-        target = slot(("z", half, dp))
-        target[...] = line(half, 1, dp).astype(BF)
-        send(("z", half, dp), target, torus.other())
+        rows = torus.rows(half, 1, dp, 0)
+        own[rows, :] = line(half, 1, dp).astype(BF)
+        send(("z", half, dp), own.at[rows], torus.other())
 
     def plane_sum(half, dp):
         return line(half, 0, dp) + arrived(("z", half, dp))
 
-    exchange = exchange_values(torus, assigned_ref, estimate_ref, moved, value_send, value_recv)
-    for plane in (1, 0):
-        multiply(plane, 2)
-        for dp in OFFSETS:
-            far(1, plane, dp)
-        far(0, plane, 2)
-        for dp in (-1, 1, 0):
-            multiply(plane, dp)
-            far(0, plane, dp)
-            if plane == 1 and dp == -1:
-                exchange(0)
-        if plane == 1:
-            for dp in OFFSETS:
-                for half in (0, 1):
-                    for d in (1, -1):
-                        near(half, 1, dp, d)
-            exchange(1)
+    def product(plane, dp):
+        multiply(plane, dp)
+        if dp == 2:
+            for other in OFFSETS:
+                far(1, plane, other)
+        far(0, plane, dp)
+
     for dp in OFFSETS:
+        product(1, dp)
+        if dp == 2:
+            exchange(0)
+    for dp in OFFSETS:
+        for half in (0, 1):
+            for d in (1, -1):
+                near(half, 1, dp, d)
+    exchange(1)
+    for dp in OFFSETS:
+        product(0, dp)
         for half in (0, 1):
             cross(half, dp)
     exchange(2)
@@ -401,20 +385,20 @@
                 near(half, 0, dp, d)
     exchange(3)
     for half in (0, 1):
-        target = slot(("pf", half))
-        target[...] = plane_sum(half, 2).astype(BF)
+        own[torus.rows(half, 0, 2, 0), :] = plane_sum(half, 2).astype(BF)
         for d in (1, -1):
             part = 0 if d == 1 else 1
-            send(("pf", half, d), target.at[pl.ds(16 * part, 16)], torus.first(half, -d))
+            block = own.at[torus.rows(half, 0, 2, 0, part)]
+            send(("pf", half, d), block, torus.first(half, -d))
     for half in (0, 1):
         for d in (1, -1):
             part = 0 if d == 1 else 1
-            target = slot(("p", half, d))
-            target[...] = plane_sum(half, -d).astype(BF)
+            rows = torus.rows(half, 0, -d, 0)
+            own[rows, :] = plane_sum(half, -d).astype(BF)
             extra = arrived(("pf", half, d))
-            rows = pl.ds(16 * part, 16)
-            target[rows, :] = (target[rows, :].astype(F32) + extra).astype(BF)
-            send(("p", half, d), target, torus.first(half, -d))
+            some = torus.rows(half, 0, -d, 0, part)
+            own[some, :] = (own[some, :].astype(F32) + extra).astype(BF)
+            send(("p", half, d), own.at[rows], torus.first(half, -d))
     for half in (0, 1):
         total = plane_sum(half, 0)
         for d in (1, -1):
@@ -425,39 +409,8 @@
         policy_ref[rows, :] = total[:, UNITS : UNITS + CHOICES]
         value_column[rows, :] = total[:, UNITS + CHOICES :]
     value_ref[...] = value_column[...].T[0:1, 0:64]
-    values_ref[...] = moved[6, :, 0:BATCH]
     for copy in started:
         copy.wait_send()
-
-
-def reduce_gradient(hidden, grads, scores, assigned, estimates):
-    quarters = sum(1 for key in KEYS if key[0] in ("qf", "pf"))
-    halves = len(KEYS) - quarters
-    return pl.pallas_call(
-        reduce_kernel,
-        out_shape=(
-            jax.ShapeDtypeStruct((64, 4, QUARTER), F32),
-            jax.ShapeDtypeStruct((64, CHOICES), F32),
-            jax.ShapeDtypeStruct((1, 64), F32),
-            jax.ShapeDtypeStruct((STEPS, BATCH), F32),
-        ),
-        in_specs=[VMEM] * 5,
-        out_specs=(VMEM,) * 4,
-        scratch_shapes=[
-            pltpu.VMEM((64, 128), F32),
-            pltpu.VMEM((10, STEPS, 128), F32),
-            pltpu.VMEM((UNITS, WIDE), BF),
-            pltpu.VMEM((46 * 32, WIDE), BF),
-            pltpu.VMEM((quarters * 16, WIDE), BF),
-            pltpu.VMEM((halves * 32, WIDE), BF),
-            pltpu.SemaphoreType.DMA((len(KEYS),)),
-            pltpu.SemaphoreType.DMA((len(KEYS),)),
-            pltpu.SemaphoreType.DMA((10,)),
-            pltpu.SemaphoreType.DMA((10,)),
-        ],
-        compiler_params=params(2),
-        name="reduce_gradient",
-    )(hidden, grads, scores, assigned, estimates)
 
 
 def actor_peers():
@@ -490,13 +443,19 @@
     return_ref,
     logprob_ref,
     action_ref,
+    assigned_ref,
+    out_ref,
+    policy_ref,
+    value_out_ref,
+    values_ref,
     hidden,
     grads,
     scores,
-    estimates,
     values,
+    value_column,
+    moved,
     held,
-    turned,
+    arena,
     factors,
     head_grad,
     gates,
@@ -515,11 +474,17 @@
     step_recv,
     back_send,
     back_recv,
+    reduce_send,
+    reduce_recv,
+    value_send,
+    value_recv,
+    ready,
 ):
     torus = Torus()
     me, peers = actor_peers()
     core, across, diagonal = peers
-    meet(torus.neighbours() + [{"actor": peer} for peer in peers])
+    far_devices = [torus.device(0, 2, 0), torus.device(0, 0, 2)]
+    meet(torus.neighbours() + far_devices + [{"actor": peer} for peer in peers])
     place = lax.axis_index("learn")
     mine = pl.ds(pl.multiple_of(place * 64, 64), 64)
     held[mine, 0:UNITS] = block_ref[...].reshape(64, UNITS)
@@ -667,7 +632,7 @@
     def step(t, carry):
         multiply(t, columns(me), True)
         stripe = pl.ds(pl.multiple_of(t * 128, 128), 128)
-        turned[:, stripe] = held[stripe, 0:UNITS].T
+        arena[:, stripe] = held[stripe, 0:UNITS].T
         arrive(t, 0)
         multiply(t, columns(core))
 
@@ -702,7 +667,6 @@
     for index in range(5):
         step_copy(STEPS, index).wait_send()
     heads(STEPS)
-    estimates[...] = jnp.concatenate([values[...], values[...]], axis=0).T[0:STEPS, 0:BATCH]
 
     carry_hidden[...] = jnp.zeros_like(carry_hidden)
     carry_cell[...] = jnp.zeros_like(carry_cell)
@@ -731,7 +695,7 @@
                 grads[t, :, pl.ds(k * QUARTER + chunk * 128, 128)] = part.astype(BF)
 
     def product(t, spot):
-        return jnp.dot(grads[t], turned[:, spot], preferred_element_type=F32)
+        return jnp.dot(grads[t], arena[:, spot], preferred_element_type=F32)
 
     def back(i, carry):
         t = STEPS - 1 - i
@@ -758,7 +722,51 @@
         return carry
 
     lax.fori_loop(0, STEPS - 1, back, 0)
+    for device in torus.neighbours():
+        pl.semaphore_signal(ready, inc=1, device_id=device, device_id_type=MESH)
     cell_back(0)
+    pl.semaphore_wait(ready, 5)
+    estimates = jnp.concatenate([values[...], values[...]], axis=0).T[0:STEPS, 0:BATCH]
+    exchange = exchange_values(torus, assigned_ref, estimates, moved, value_send, value_recv)
+    reduce_blocks(
+        torus,
+        hidden,
+        grads,
+        scores,
+        exchange,
+        out_ref,
+        policy_ref,
+        value_out_ref,
+        value_column,
+        held,
+        arena,
+        reduce_send,
+        reduce_recv,
+    )
+    values_ref[...] = moved[6, :, 0:BATCH]
+
+
+RESULTS = (
+    jax.ShapeDtypeStruct((64, 4, QUARTER), F32),
+    jax.ShapeDtypeStruct((64, CHOICES), F32),
+    jax.ShapeDtypeStruct((1, 64), F32),
+    jax.ShapeDtypeStruct((STEPS, BATCH), F32),
+)
+
+
+def hand_on_kernel(*refs):
+    for source, target in zip(refs[:4], refs[4:]):
+        target[...] = source[...]
+
+
+def hand_on(*results):
+    return pl.pallas_call(
+        hand_on_kernel,
+        out_shape=RESULTS,
+        in_specs=[VMEM] * 4,
+        out_specs=(VMEM,) * 4,
+        name="hand_on",
+    )(*results)
 
 
 def train(*operands):
@@ -766,18 +774,18 @@
     specs[5] = pl.BlockSpec(memory_space=pltpu.SMEM)
     return pl.pallas_call(
         train_kernel,
-        out_shape=(
-            jax.ShapeDtypeStruct((STEPS + 1, BATCH, UNITS), BF),
-            jax.ShapeDtypeStruct((STEPS, BATCH, UNITS), BF),
-            jax.ShapeDtypeStruct((STEPS + 1, BATCH, 2 * CHOICES), BF),
-            jax.ShapeDtypeStruct((STEPS, BATCH), F32),
-        ),
+        out_shape=RESULTS,
         in_specs=specs,
         out_specs=(VMEM,) * 4,
         scratch_shapes=[
+            pltpu.VMEM((STEPS + 1, BATCH, UNITS), BF),
+            pltpu.VMEM((STEPS, BATCH, UNITS), BF),
+            pltpu.VMEM((STEPS + 1, BATCH, 2 * CHOICES), BF),
             pltpu.VMEM((BATCH, 128), F32),
+            pltpu.VMEM((64, 128), F32),
+            pltpu.VMEM((10, STEPS, 128), F32),
             pltpu.VMEM((UNITS, WIDE), BF),
-            pltpu.VMEM((UNITS, UNITS), BF),
+            pltpu.VMEM((UNITS, WIDE), BF),
             pltpu.VMEM((STEPS, 6, BATCH, QUARTER), BF),
             pltpu.VMEM((STEPS + 1, BATCH, QUARTER), F32),
             pltpu.VMEM((STEPS, BATCH, UNITS), BF),
@@ -796,6 +804,11 @@
             pltpu.SemaphoreType.DMA((STEPS + 1, 5)),
             pltpu.SemaphoreType.DMA((STEPS, 5)),
             pltpu.SemaphoreType.DMA((STEPS, 5)),
+            pltpu.SemaphoreType.DMA((len(KEYS),)),
+            pltpu.SemaphoreType.DMA((len(KEYS),)),
+            pltpu.SemaphoreType.DMA((10,)),
+            pltpu.SemaphoreType.DMA((10,)),
+            pltpu.SemaphoreType.REGULAR,
         ],
         compiler_params=params(1),
         name="train",
@@ -816,7 +829,7 @@
     segment_counts,
     assignment,
 ):
-    hidden, grads, scores, estimates = train(
+    results = train(
         rec_weight,
         head_weight,
         value_head[None],
@@ -828,10 +841,9 @@
         returns[0].T,
         old_logprob[0].T,
         taken_action[0].T,
+        assignment,
     )
-    rec_share, policy_share, value_share, values = reduce_gradient(
-        hidden, grads, scores, assignment, estimates
-    )
+    rec_share, policy_share, value_share, values = hand_on(*results)
     return (rec_share, policy_share, value_share[0], values.T[None])
 
 

time: 285 us -> 271 us (0.951)
  Pallas kernels: 278 us -> 270 us
  local copies, waits for them, and re-layouts: 5.66 us -> 0 us
    pallas_call x2, Pallas kernels: 278 us -> 270 us  [the longest x1 268 us: train(): pl.pallas_call(train_kernel, out_shape=RESULTS, in_specs=specs, out_specs...]
    unnamed x4 -> x0, local copies, waits for them, and re-layouts: 5.66 us -> none
where the time goes in v4:
time: 271 us
  Pallas kernels  270 us (100%)
    pallas_call x1, Pallas kernels, train(): pl.pallas_call(train_kernel, out_shape=RESULTS, in_specs=specs, out_specs...  268 us

profile of v4, /device:TPU:0, one launch (start us, length us, event | category | flops | bytes accessed | tf_op | source)
XLA Modules:
  0.0 270.8 jit_solution(18408238850133407594)
XLA Ops:
  0.6 268.2 %train.1 = (f32[64,4,512]{2,1,0:T(4,128)}, f32[64,128]{1,0:T(8,128)}, f32[1,64]{1,0:T(1,128)}, f32[16,64]{1,0:T(8,128)}) custom-call(bf16[64,4,512]{2,1,0:T(4,128)(2,1)} %block_ref.1, bf16[64,128]{1,0:T(8,128)(2,1)} %head_ref.1, bf16[1,64]{1,0:T(2,128)(2,1)} %bitcast.29, bf16[64,16,4,512]{3,2,1,0:T(4,128)(2,1)} %bitcast.22, bf16[64,2,512]{2,1,0:T(2,128)(2,1)} %bitcast.23, ...), custom_call_target="tpu_custom_call" | custom-call | tf_op jit(solution)/shard_map/train/pallas_call | solution.py:775
  268.9 1.9 hand_on.1

commit v5 on v4

--- a/solution.py
+++ b/solution.py
@@ -13,7 +13,7 @@
 BATCH = 64
 STEPS = 16
 CHOICES = 128
-WIDE = UNITS + 2 * CHOICES
+PAIR = 2 * CHOICES
 VMEM = pl.BlockSpec(memory_space=pltpu.VMEM)
 LIMIT = 60 * 2**20
 OFFSETS = (2, -1, 1, 0)
@@ -30,6 +30,10 @@
     for device in devices:
         pl.semaphore_signal(barrier, inc=1, device_id=device, device_id_type=MESH)
     pl.semaphore_wait(barrier, len(devices))
+
+
+GATHER_AT = (0, 1, 3, 8)
+REDUCE_AT = (8, 11, 13)
 
 
 class Torus:
@@ -258,12 +262,8 @@
     torus,
     hidden,
     grads,
-    scores,
     exchange,
     out_ref,
-    policy_ref,
-    value_ref,
-    value_column,
     own,
     arena,
     send_sems,
@@ -320,12 +320,6 @@
                 (((0,), (0,)), ((), ())),
                 preferred_element_type=F32,
             ).astype(BF)
-        own[spot, UNITS:WIDE] = lax.dot_general(
-            hidden[1 : STEPS + 1, :, spot].reshape(STEPS * BATCH, 256),
-            scores[1 : STEPS + 1].reshape(STEPS * BATCH, 2 * CHOICES),
-            (((0,), (0,)), ((), ())),
-            preferred_element_type=F32,
-        ).astype(BF)
 
     def far(half, plane, dp):
         for d in (1, -1):
@@ -406,11 +400,101 @@
         rows = pl.ds(32 * half, 32)
         for k in range(4):
             out_ref[rows, k, :] = total[:, k * QUARTER : (k + 1) * QUARTER]
-        policy_ref[rows, :] = total[:, UNITS : UNITS + CHOICES]
-        value_column[rows, :] = total[:, UNITS + CHOICES :]
-    value_ref[...] = value_column[...].T[0:1, 0:64]
     for copy in started:
         copy.wait_send()
+
+
+class Heads:
+    def __init__(self, torus, held, partial, along_x, along_y, along_z, sems):
+        self.torus, self.held, self.partial = torus, held, partial
+        self.along = (along_z, along_y, along_x)
+        self.sems = sems
+
+    def group(self, plane, dx):
+        first = self.torus.device(plane, dx, 0)["learn"] // 4
+        return pl.ds(pl.multiple_of(first * 256, 256), 256)
+
+    def block(self, plane, dx, dy):
+        return pl.ds(pl.multiple_of(self.torus.device(plane, dx, dy)["learn"] * 64, 64), 64)
+
+    def copy(self, way, index, source, target, device):
+        return pltpu.make_async_remote_copy(
+            src_ref=source,
+            dst_ref=target,
+            send_sem=self.sems[2 * way].at[index],
+            recv_sem=self.sems[2 * way + 1].at[index],
+            device_id=device,
+            device_id_type=MESH,
+        )
+
+    def gather_copies(self, stage, arrivals):
+        held, torus, result = self.held, self.torus, []
+        if stage == 0:
+            rows = self.block(1 if arrivals else 0, 0, 0)
+            result.append(self.copy(0, 0, held.at[rows], held.at[rows], torus.other()))
+        for d in (1, 2, 3):
+            for plane in (0, 1):
+                index = 1 + (stage - 1) * 6 + (d - 1) * 2 + plane
+                shift = 4 - d if arrivals else 0
+                if stage == 1:
+                    rows = self.block(plane, 0, shift)
+                    device = torus.device(0, 0, d)
+                elif stage == 2:
+                    rows = self.group(plane, shift)
+                    device = torus.device(0, d, 0)
+                else:
+                    continue
+                result.append(self.copy(0, index, held.at[rows], held.at[rows], device))
+        return result
+
+    def gather(self, stage):
+        if stage > 0:
+            for copy in self.gather_copies(stage - 1, True):
+                copy.wait_recv()
+            for copy in self.gather_copies(stage - 1, False):
+                copy.wait_send()
+        if stage < 3:
+            for copy in self.gather_copies(stage, False):
+                copy.start()
+
+    def reduce_copies(self, stage):
+        partial, torus, result = self.partial, self.torus, []
+        along_z, along_y, along_x = self.along
+        if stage == 2:
+            rows = self.block(1, 0, 0)
+            result.append(self.copy(1, 12, partial.at[rows], along_z, torus.other()))
+        for d in (1, 2, 3):
+            for plane in (0, 1):
+                slot = (d - 1) * 2 + plane
+                if stage == 0:
+                    rows, target = self.group(plane, d), along_x.at[slot]
+                    device = torus.device(0, d, 0)
+                elif stage == 1:
+                    rows, target = self.block(plane, 0, d), along_y.at[slot]
+                    device = torus.device(0, 0, d)
+                else:
+                    continue
+                result.append(self.copy(1, stage * 6 + slot, partial.at[rows], target, device))
+        return result
+
+    def reduce(self, stage):
+        along_z, along_y, along_x = self.along
+        if stage > 0:
+            for copy in self.reduce_copies(stage - 1):
+                copy.wait()
+        if stage in (1, 2):
+            for plane in (0, 1):
+                rows = self.group(plane, 0) if stage == 1 else self.block(plane, 0, 0)
+                arrived = along_x if stage == 1 else along_y
+                total = self.partial[rows, :].astype(F32)
+                for d in (1, 2, 3):
+                    total = total + arrived[(d - 1) * 2 + plane].astype(F32)
+                self.partial[rows, :] = total.astype(BF)
+        if stage < 3:
+            for copy in self.reduce_copies(stage):
+                copy.start()
+            return None
+        return self.partial[self.block(0, 0, 0), :].astype(F32) + along_z[...].astype(F32)
 
 
 def actor_peers():
@@ -421,7 +505,7 @@
 
 
 def columns(quarter, start=0, size=QUARTER):
-    return pl.ds(pl.multiple_of(quarter * QUARTER + start, min(size, 256)), size)
+    return pl.ds(pl.multiple_of(quarter * QUARTER + start, 128), size)
 
 
 def sigmoid(value):
@@ -429,6 +513,9 @@
 
 
 HALF = QUARTER // 2
+DIRECT = 384
+SUMMED = QUARTER - DIRECT
+WIDTHS = (DIRECT, DIRECT, SUMMED, SUMMED)
 
 
 def train_kernel(
@@ -452,7 +539,11 @@
     grads,
     scores,
     values,
-    value_column,
+    heads_held,
+    heads_partial,
+    heads_x,
+    heads_y,
+    heads_z,
     moved,
     held,
     arena,
@@ -479,6 +570,7 @@
     value_send,
     value_recv,
     ready,
+    *heads_sems,
 ):
     torus = Torus()
     me, peers = actor_peers()
@@ -487,10 +579,11 @@
     meet(torus.neighbours() + far_devices + [{"actor": peer} for peer in peers])
     place = lax.axis_index("learn")
     mine = pl.ds(pl.multiple_of(place * 64, 64), 64)
-    held[mine, 0:UNITS] = block_ref[...].reshape(64, UNITS)
-    held[mine, UNITS : UNITS + CHOICES] = head_ref[...]
+    held[mine, :] = block_ref[...].reshape(64, UNITS)
+    heads_held[mine, 0:CHOICES] = head_ref[...]
     line = jnp.concatenate([value_ref[...].astype(F32), jnp.zeros((1, 64), F32)], axis=1)
-    held[mine, UNITS + CHOICES : WIDE] = jnp.broadcast_to(line, (128, 128)).T[0:64].astype(BF)
+    heads_held[mine, CHOICES:PAIR] = jnp.broadcast_to(line, (128, 128)).T[0:64].astype(BF)
+    heads_moves = Heads(torus, heads_held, heads_partial, heads_x, heads_y, heads_z, heads_sems)
 
     def pieces(t):
         return (
@@ -548,7 +641,7 @@
 
     def heads(index):
         t = index - 1
-        result = jnp.dot(hidden[index], held[:, UNITS:WIDE], preferred_element_type=F32)
+        result = jnp.dot(hidden[index], heads_held[...], preferred_element_type=F32)
         logits = result[:, 0:CHOICES]
         estimate = result[:, CHOICES : CHOICES + 1]
         share = aux[:, 80:81]
@@ -568,7 +661,7 @@
         values[...] = jnp.where(lane == t, estimate * live, values[...])
         head_grad[index] = lax.dot_general(
             scores[index],
-            held[columns(me), UNITS:WIDE],
+            heads_held[columns(me), :],
             (((1,), (1,)), ((), ())),
             preferred_element_type=F32,
         )
@@ -632,13 +725,20 @@
     def step(t, carry):
         multiply(t, columns(me), True)
         stripe = pl.ds(pl.multiple_of(t * 128, 128), 128)
-        arena[:, stripe] = held[stripe, 0:UNITS].T
+        arena[:, stripe] = held[stripe, :].T
         arrive(t, 0)
         multiply(t, columns(core))
 
-        @pl.when(t >= 2)
+        for stage, when in enumerate(GATHER_AT):
+
+            @pl.when(t == when)
+            def _(stage=stage):
+                heads_moves.gather(stage)
+
+        @pl.when(t > GATHER_AT[3])
         def _():
-            heads(t - 1)
+            heads(2 * (t - GATHER_AT[3]) - 1)
+            heads(2 * (t - GATHER_AT[3]))
 
         arrive(t, 1)
         step_copy(t, 4).start()
@@ -675,8 +775,8 @@
 
     def back_copy(t, index):
         return pltpu.make_async_remote_copy(
-            src_ref=sent_core.at[t] if index == 4 else sent.at[t, index],
-            dst_ref=got_core.at[t] if index == 4 else got.at[t, index],
+            src_ref=sent_core.at[t] if index == 4 else sent.at[t, index, :, pl.ds(0, WIDTHS[index])],
+            dst_ref=got_core.at[t] if index == 4 else got.at[t, index, :, pl.ds(0, WIDTHS[index])],
             send_sem=back_send.at[t, index],
             recv_sem=back_recv.at[t, index],
             device_id={"actor": targets[index]},
@@ -700,23 +800,41 @@
     def back(i, carry):
         t = STEPS - 1 - i
         cell_back(t)
-        for index, quarter, start in ((2, diagonal, HALF), (0, diagonal, 0), (1, across, 0)):
-            sent[t, index] = product(t, columns(quarter, start, HALF)).astype(BF)
+        for index, quarter, start in ((2, diagonal, DIRECT), (0, diagonal, 0), (1, across, 0)):
+            width = WIDTHS[index]
+            sent[t, index, :, 0:width] = product(t, columns(quarter, start, width)).astype(BF)
             back_copy(t, index).start()
-        part = product(t, columns(across, HALF, HALF))
+        part = product(t, columns(across, DIRECT, SUMMED))
         sent_core[t] = product(t, columns(core)).astype(BF)
         back_copy(t, 4).start()
         back_copy(t, 2).wait_recv()
-        sent[t, 3] = (part + got[t, 2].astype(F32)).astype(BF)
+        sent[t, 3, :, 0:SUMMED] = (part + got[t, 2, :, 0:SUMMED].astype(F32)).astype(BF)
         back_copy(t, 3).start()
         carry_hidden[...] = product(t, columns(me))
+
+        @pl.when(i < 8)
+        def _():
+            spot = pl.ds(pl.multiple_of(i * 256, 256), 256)
+            heads_partial[spot, :] = lax.dot_general(
+                hidden[1 : STEPS + 1, :, spot].reshape(STEPS * BATCH, 256),
+                scores[1 : STEPS + 1].reshape(STEPS * BATCH, PAIR),
+                (((0,), (0,)), ((), ())),
+                preferred_element_type=F32,
+            ).astype(BF)
+
+        for stage, when in enumerate(REDUCE_AT):
+
+            @pl.when(i == when)
+            def _(stage=stage):
+                heads_moves.reduce(stage)
+
         back_copy(t, 4).wait_recv()
         carry_hidden[...] += got_core[t].astype(F32)
         for index in (0, 1):
             back_copy(t, index).wait_recv()
-        carry_hidden[:, 0:HALF] += got[t, 0].astype(F32) + got[t, 1].astype(F32)
+        carry_hidden[:, 0:DIRECT] += got[t, 0, :, 0:DIRECT].astype(F32) + got[t, 1, :, 0:DIRECT].astype(F32)
         back_copy(t, 3).wait_recv()
-        carry_hidden[:, HALF:QUARTER] += got[t, 3].astype(F32)
+        carry_hidden[:, DIRECT:QUARTER] += got[t, 3, :, 0:SUMMED].astype(F32)
         for index in range(5):
             back_copy(t, index).wait_send()
         return carry
@@ -725,6 +843,9 @@
     for device in torus.neighbours():
         pl.semaphore_signal(ready, inc=1, device_id=device, device_id_type=MESH)
     cell_back(0)
+    heads_total = heads_moves.reduce(3)
+    policy_ref[...] = heads_total[:, 0:CHOICES]
+    value_out_ref[...] = heads_total[:, CHOICES:PAIR].T[0:1, 0:64]
     pl.semaphore_wait(ready, 5)
     estimates = jnp.concatenate([values[...], values[...]], axis=0).T[0:STEPS, 0:BATCH]
     exchange = exchange_values(torus, assigned_ref, estimates, moved, value_send, value_recv)
@@ -732,12 +853,8 @@
         torus,
         hidden,
         grads,
-        scores,
         exchange,
         out_ref,
-        policy_ref,
-        value_out_ref,
-        value_column,
         held,
         arena,
         reduce_send,
@@ -782,10 +899,14 @@
             pltpu.VMEM((STEPS, BATCH, UNITS), BF),
             pltpu.VMEM((STEPS + 1, BATCH, 2 * CHOICES), BF),
             pltpu.VMEM((BATCH, 128), F32),
-            pltpu.VMEM((64, 128), F32),
+            pltpu.VMEM((UNITS, PAIR), BF),
+            pltpu.VMEM((UNITS, PAIR), BF),
+            pltpu.VMEM((6, 256, PAIR), BF),
+            pltpu.VMEM((6, 64, PAIR), BF),
+            pltpu.VMEM((64, PAIR), BF),
             pltpu.VMEM((10, STEPS, 128), F32),
-            pltpu.VMEM((UNITS, WIDE), BF),
-            pltpu.VMEM((UNITS, WIDE), BF),
+            pltpu.VMEM((UNITS, UNITS), BF),
+            pltpu.VMEM((UNITS, UNITS), BF),
             pltpu.VMEM((STEPS, 6, BATCH, QUARTER), BF),
             pltpu.VMEM((STEPS + 1, BATCH, QUARTER), F32),
             pltpu.VMEM((STEPS, BATCH, UNITS), BF),
@@ -794,8 +915,8 @@
             pltpu.VMEM((BATCH, QUARTER), F32),
             pltpu.VMEM((BATCH, QUARTER), F32),
             pltpu.VMEM((BATCH, QUARTER), F32),
-            pltpu.VMEM((STEPS, 4, BATCH, HALF), BF),
-            pltpu.VMEM((STEPS, 4, BATCH, HALF), BF),
+            pltpu.VMEM((STEPS, 4, BATCH, max(DIRECT, SUMMED)), BF),
+            pltpu.VMEM((STEPS, 4, BATCH, max(DIRECT, SUMMED)), BF),
             pltpu.VMEM((STEPS, BATCH, QUARTER), BF),
             pltpu.VMEM((STEPS, BATCH, QUARTER), BF),
             pltpu.SemaphoreType.DMA((len(KEYS),)),
@@ -809,6 +930,10 @@
             pltpu.SemaphoreType.DMA((10,)),
             pltpu.SemaphoreType.DMA((10,)),
             pltpu.SemaphoreType.REGULAR,
+            pltpu.SemaphoreType.DMA((13,)),
+            pltpu.SemaphoreType.DMA((13,)),
+            pltpu.SemaphoreType.DMA((13,)),
+            pltpu.SemaphoreType.DMA((13,)),
         ],
         compiler_params=params(1),
         name="train",

time: 271 us -> 259 us (0.956)
  Pallas kernels: 270 us -> 258 us
    pallas_call x1, Pallas kernels: 268 us -> 256 us  [train(): pl.pallas_call(train_kernel, out_shape=RESULTS, in_specs=specs, out_specs...]
where the time goes in v5:
time: 259 us
  Pallas kernels  258 us (100%)
    pallas_call x1, Pallas kernels, train(): pl.pallas_call(train_kernel, out_shape=RESULTS, in_specs=specs, out_specs...  256 us

profile of v5, /device:TPU:0, one launch (start us, length us, event | category | flops | bytes accessed | tf_op | source)
XLA Modules:
  0.0 258.7 jit_solution(2550262915890568191)
XLA Ops:
  0.6 256.1 %train.1 = (f32[64,4,512]{2,1,0:T(4,128)}, f32[64,128]{1,0:T(8,128)}, f32[1,64]{1,0:T(1,128)}, f32[16,64]{1,0:T(8,128)}) custom-call(bf16[64,4,512]{2,1,0:T(4,128)(2,1)} %block_ref.1, bf16[64,128]{1,0:T(8,128)(2,1)} %head_ref.1, bf16[1,64]{1,0:T(2,128)(2,1)} %bitcast.29, bf16[64,16,4,512]{3,2,1,0:T(4,128)(2,1)} %bitcast.22, bf16[64,2,512]{2,1,0:T(2,128)(2,1)} %bitcast.23, ...), custom_call_target="tpu_custom_call" | custom-call | tf_op jit(solution)/shard_map/train/pallas_call | solution.py:892
  256.8 1.9 hand_on.1

commit v6 on v5

--- a/solution.py
+++ b/solution.py
@@ -513,16 +513,13 @@
 
 
 HALF = QUARTER // 2
-DIRECT = 384
-SUMMED = QUARTER - DIRECT
-WIDTHS = (DIRECT, DIRECT, SUMMED, SUMMED)
 
 
 def train_kernel(
     block_ref,
     head_ref,
     value_ref,
-    gate_ref,
+    gate_source,
     state_ref,
     counts_ref,
     start_ref,
@@ -557,8 +554,6 @@
     carry_cell,
     sent,
     got,
-    sent_core,
-    got_core,
     gather_send,
     gather_recv,
     step_send,
@@ -570,8 +565,12 @@
     value_send,
     value_recv,
     ready,
+    gate_ref,
+    gate_sem,
     *heads_sems,
 ):
+    gate_copy = pltpu.make_async_copy(gate_source, gate_ref, gate_sem)
+    gate_copy.start()
     torus = Torus()
     me, peers = actor_peers()
     core, across, diagonal = peers
@@ -718,6 +717,8 @@
     aux[...] = jnp.where(lane < 80, table.T[0:BATCH], live)
 
     def unpack(t):
+        if t == 0:
+            gate_copy.wait()
         gates[t] = gate_ref[:, t].reshape(BATCH, UNITS)
 
     gather_blocks(held, gather_send, gather_recv, unpack)
@@ -771,12 +772,12 @@
     carry_hidden[...] = jnp.zeros_like(carry_hidden)
     carry_cell[...] = jnp.zeros_like(carry_cell)
 
-    targets = (diagonal, across, core, across, core)
+    targets = (diagonal, across, core)
 
     def back_copy(t, index):
         return pltpu.make_async_remote_copy(
-            src_ref=sent_core.at[t] if index == 4 else sent.at[t, index, :, pl.ds(0, WIDTHS[index])],
-            dst_ref=got_core.at[t] if index == 4 else got.at[t, index, :, pl.ds(0, WIDTHS[index])],
+            src_ref=sent.at[t, index],
+            dst_ref=got.at[t, index],
             send_sem=back_send.at[t, index],
             recv_sem=back_recv.at[t, index],
             device_id={"actor": targets[index]},
@@ -800,16 +801,9 @@
     def back(i, carry):
         t = STEPS - 1 - i
         cell_back(t)
-        for index, quarter, start in ((2, diagonal, DIRECT), (0, diagonal, 0), (1, across, 0)):
-            width = WIDTHS[index]
-            sent[t, index, :, 0:width] = product(t, columns(quarter, start, width)).astype(BF)
+        for index in range(3):
+            sent[t, index] = product(t, columns(targets[index])).astype(BF)
             back_copy(t, index).start()
-        part = product(t, columns(across, DIRECT, SUMMED))
-        sent_core[t] = product(t, columns(core)).astype(BF)
-        back_copy(t, 4).start()
-        back_copy(t, 2).wait_recv()
-        sent[t, 3, :, 0:SUMMED] = (part + got[t, 2, :, 0:SUMMED].astype(F32)).astype(BF)
-        back_copy(t, 3).start()
         carry_hidden[...] = product(t, columns(me))
 
         @pl.when(i < 8)
@@ -828,14 +822,10 @@
             def _(stage=stage):
                 heads_moves.reduce(stage)
 
-        back_copy(t, 4).wait_recv()
-        carry_hidden[...] += got_core[t].astype(F32)
-        for index in (0, 1):
+        for index in (2, 0, 1):
             back_copy(t, index).wait_recv()
-        carry_hidden[:, 0:DIRECT] += got[t, 0, :, 0:DIRECT].astype(F32) + got[t, 1, :, 0:DIRECT].astype(F32)
-        back_copy(t, 3).wait_recv()
-        carry_hidden[:, DIRECT:QUARTER] += got[t, 3, :, 0:SUMMED].astype(F32)
-        for index in range(5):
+            carry_hidden[...] += got[t, index].astype(F32)
+        for index in range(3):
             back_copy(t, index).wait_send()
         return carry
 
@@ -889,6 +879,7 @@
 def train(*operands):
     specs = [VMEM] * len(operands)
     specs[5] = pl.BlockSpec(memory_space=pltpu.SMEM)
+    specs[3] = pl.BlockSpec(memory_space=pl.ANY)
     return pl.pallas_call(
         train_kernel,
         out_shape=RESULTS,
@@ -915,21 +906,21 @@
             pltpu.VMEM((BATCH, QUARTER), F32),
             pltpu.VMEM((BATCH, QUARTER), F32),
             pltpu.VMEM((BATCH, QUARTER), F32),
-            pltpu.VMEM((STEPS, 4, BATCH, max(DIRECT, SUMMED)), BF),
-            pltpu.VMEM((STEPS, 4, BATCH, max(DIRECT, SUMMED)), BF),
-            pltpu.VMEM((STEPS, BATCH, QUARTER), BF),
-            pltpu.VMEM((STEPS, BATCH, QUARTER), BF),
+            pltpu.VMEM((STEPS, 3, BATCH, QUARTER), BF),
+            pltpu.VMEM((STEPS, 3, BATCH, QUARTER), BF),
             pltpu.SemaphoreType.DMA((len(KEYS),)),
             pltpu.SemaphoreType.DMA((len(KEYS),)),
             pltpu.SemaphoreType.DMA((STEPS + 1, 5)),
             pltpu.SemaphoreType.DMA((STEPS + 1, 5)),
-            pltpu.SemaphoreType.DMA((STEPS, 5)),
-            pltpu.SemaphoreType.DMA((STEPS, 5)),
+            pltpu.SemaphoreType.DMA((STEPS, 3)),
+            pltpu.SemaphoreType.DMA((STEPS, 3)),
             pltpu.SemaphoreType.DMA((len(KEYS),)),
             pltpu.SemaphoreType.DMA((len(KEYS),)),
             pltpu.SemaphoreType.DMA((10,)),
             pltpu.SemaphoreType.DMA((10,)),
             pltpu.SemaphoreType.REGULAR,
+            pltpu.VMEM((BATCH, STEPS, 4, QUARTER), BF),
+            pltpu.SemaphoreType.DMA(()),
             pltpu.SemaphoreType.DMA((13,)),
             pltpu.SemaphoreType.DMA((13,)),
             pltpu.SemaphoreType.DMA((13,)),

time: 259 us -> 254 us (0.981)
  Pallas kernels: 258 us -> 253 us
    pallas_call x1, Pallas kernels: 256 us -> 251 us  [train(): pl.pallas_call(train_kernel, out_shape=RESULTS, in_specs=specs, out_specs...]
where the time goes in v6:
time: 254 us
  Pallas kernels  253 us (100%)
    pallas_call x1, Pallas kernels, train(): pl.pallas_call(train_kernel, out_shape=RESULTS, in_specs=specs, out_specs...  251 us

profile of v6, /device:TPU:0, one launch (start us, length us, event | category | flops | bytes accessed | tf_op | source)
XLA Modules:
  0.0 253.6 jit_solution(17163992391112578806)
XLA Ops:
  0.6 251.1 %train.1 = (f32[64,4,512]{2,1,0:T(4,128)}, f32[64,128]{1,0:T(8,128)}, f32[1,64]{1,0:T(1,128)}, f32[16,64]{1,0:T(8,128)}) custom-call(bf16[64,4,512]{2,1,0:T(4,128)(2,1)} %block_ref.1, bf16[64,128]{1,0:T(8,128)(2,1)} %head_ref.1, bf16[1,64]{1,0:T(2,128)(2,1)} %bitcast.29, bf16[64,16,4,512]{3,2,1,0:T(4,128)(2,1)} %bitcast.22, bf16[64,2,512]{2,1,0:T(2,128)(2,1)} %bitcast.23, ...), custom_call_target="tpu_custom_call" | custom-call | tf_op jit(solution)/shard_map/train/pallas_call | solution.py:883
  251.7 1.9 hand_on.1

commit v7 on v6

--- a/solution.py
+++ b/solution.py
@@ -80,6 +80,7 @@
         keys += [("p", half, d) for d in (1, -1)]
         keys += [("pf", half, d) for d in (1, -1)]
         keys += [("z", half, dp) for dp in OFFSETS]
+        keys += [("zq", half)]
         for plane in (0, 1):
             for dp in OFFSETS:
                 keys += [("q", half, plane, dp, d) for d in (1, -1)]
@@ -123,11 +124,12 @@
         for d in (1, -1):
             part = 0 if d == 1 else 1
             arrive(("q", half, plane, dp, d), torus.rows(half, plane, dp, -d))
-            send(
-                ("qf", half, plane, dp, d),
-                torus.rows(half, plane, dp, -d, part),
-                torus.second(half, d),
-            )
+            if (plane, dp) != (1, 0):
+                send(
+                    ("qf", half, plane, dp, d),
+                    torus.rows(half, plane, dp, -d, part),
+                    torus.second(half, d),
+                )
 
     def cross(half, dp):
         send(("z", half, dp), torus.rows(half, 0, dp, 0), torus.other())
@@ -174,6 +176,11 @@
     for half in (0, 1):
         pass_on(half, 1, 0)
     for half in (0, 1):
+        for d in (1, -1):
+            part = 0 if d == 1 else 1
+            arrive(("qf", half, 0, 0, d), torus.rows(half, 0, 0, -2 * d, part))
+        send(("zq", half), torus.rows(half, 0, 0, 2), torus.other())
+    for half in (0, 1):
         pass_on(half, 0, 2)
     for half in (0, 1):
         for d in (1, -1):
@@ -182,12 +189,13 @@
         pass_on(half, 1, 2)
     for half in (0, 1):
         for plane in (0, 1):
-            for dp in OFFSETS:
+            for dp in (2, -1, 1):
                 for d in (1, -1):
                     part = 0 if d == 1 else 1
                     arrive(
                         ("qf", half, plane, dp, d), torus.rows(half, plane, dp, -2 * d, part)
                     )
+        arrive(("zq", half), torus.rows(half, 1, 0, 2))
     for copy in started:
         copy.wait_send()
 
@@ -772,12 +780,13 @@
     carry_hidden[...] = jnp.zeros_like(carry_hidden)
     carry_cell[...] = jnp.zeros_like(carry_cell)
 
-    targets = (diagonal, across, core)
+    targets = (diagonal, diagonal, across, across, core)
+    spans = ((0, HALF), (HALF, HALF), (0, HALF), (HALF, HALF), (0, QUARTER))
 
     def back_copy(t, index):
         return pltpu.make_async_remote_copy(
-            src_ref=sent.at[t, index],
-            dst_ref=got.at[t, index],
+            src_ref=sent.at[t, index // 2, :, pl.ds(*spans[index])],
+            dst_ref=got.at[t, index // 2, :, pl.ds(*spans[index])],
             send_sem=back_send.at[t, index],
             recv_sem=back_recv.at[t, index],
             device_id={"actor": targets[index]},
@@ -801,8 +810,9 @@
     def back(i, carry):
         t = STEPS - 1 - i
         cell_back(t)
-        for index in range(3):
-            sent[t, index] = product(t, columns(targets[index])).astype(BF)
+        for index, (first, size) in enumerate(spans):
+            part = product(t, columns(targets[index], first, size)).astype(BF)
+            sent[t, index // 2, :, pl.ds(first, size)] = part
             back_copy(t, index).start()
         carry_hidden[...] = product(t, columns(me))
 
@@ -822,10 +832,11 @@
             def _(stage=stage):
                 heads_moves.reduce(stage)
 
-        for index in (2, 0, 1):
+        for index in (4, 0, 1, 2, 3):
             back_copy(t, index).wait_recv()
-            carry_hidden[...] += got[t, index].astype(F32)
-        for index in range(3):
+            spot = pl.ds(*spans[index])
+            carry_hidden[:, spot] += got[t, index // 2, :, spot].astype(F32)
+        for index in range(5):
             back_copy(t, index).wait_send()
         return carry
 
@@ -912,8 +923,8 @@
             pltpu.SemaphoreType.DMA((len(KEYS),)),
             pltpu.SemaphoreType.DMA((STEPS + 1, 5)),
             pltpu.SemaphoreType.DMA((STEPS + 1, 5)),
-            pltpu.SemaphoreType.DMA((STEPS, 3)),
-            pltpu.SemaphoreType.DMA((STEPS, 3)),
+            pltpu.SemaphoreType.DMA((STEPS, 5)),
+            pltpu.SemaphoreType.DMA((STEPS, 5)),
             pltpu.SemaphoreType.DMA((len(KEYS),)),
             pltpu.SemaphoreType.DMA((len(KEYS),)),
             pltpu.SemaphoreType.DMA((10,)),

time: 254 us -> 255 us (level)
  no operation moved by 1% of the time
where the time goes in v7:
time: 255 us
  Pallas kernels  254 us (100%)
    pallas_call x1, Pallas kernels, train(): pl.pallas_call(train_kernel, out_shape=RESULTS, in_specs=specs, out_specs...  252 us

profile of v7, /device:TPU:0, one launch (start us, length us, event | category | flops | bytes accessed | tf_op | source)
XLA Modules:
  0.0 254.7 jit_solution(1463365267526124389)
XLA Ops:
  0.6 252.2 %train.1 = (f32[64,4,512]{2,1,0:T(4,128)}, f32[64,128]{1,0:T(8,128)}, f32[1,64]{1,0:T(1,128)}, f32[16,64]{1,0:T(8,128)}) custom-call(bf16[64,4,512]{2,1,0:T(4,128)(2,1)} %block_ref.1, bf16[64,128]{1,0:T(8,128)(2,1)} %head_ref.1, bf16[1,64]{1,0:T(2,128)(2,1)} %bitcast.29, bf16[64,16,4,512]{3,2,1,0:T(4,128)(2,1)} %bitcast.22, bf16[64,2,512]{2,1,0:T(2,128)(2,1)} %bitcast.23, ...), custom_call_target="tpu_custom_call" | custom-call | tf_op jit(solution)/shard_map/train/pallas_call | solution.py:894
  252.8 1.9 hand_on.1
